TPU v7x, 512 devices: a whole 4x8x8 slice. The times are simulated.
512 devices in a mesh: grp: 16 (over y, core), se: 32 (over x, z).
Axes of the slice: x: 4, y: 8, z: 8, core: 2. Of those that a mesh axis runs over, the one named last changes fastest.
Arguments:
- pressure: bfloat16 [12288, 64, 128], P(('grp', 'se')), may hold values from -6 to 6
- block_owner: int32 [12288], P(('grp', 'se')), may hold values from 0 to 31, as said below
- level_one: bfloat16 [512, 256, 6144], P(('grp', 'se')), may hold values from -0.078125 to 0.078125
- level_one_map: int32 [512, 256], P(('grp', 'se')), may hold values from 0 to 4095, as said below
- level_two: bfloat16 [16, 128, 4096], P('grp', None, 'se'), may hold values from -0.375 to 0.375
- level_two_map: int32 [16, 16, 128], P('grp'), may hold values from 0 to 4095
Outputs:
- level_two_load: float32 [16, 64, 4096], P('grp', None, 'se')
- root_load: float32 [64, 4096], P(None, ('grp', 'se'))
Inputs may be any that keep to these rules, and one draw needn't show every extreme that they name: `block_owner`: in each group (32 devices of 24 blocks each) one device holds at most 2 blocks for one superelement, and at most 48 blocks load one superelement; both bounds are reached in every group. `level_one_map`: for each first-level superelement, at most 16 of its boundary degrees of freedom map into one block j * 128 to (j + 1) * 128 - 1 of the group interior, and exactly 16 do for some block, for every superelement.
All inputs are finite; a program needn't handle non-finite values.
Results may differ from a plain program's by a relative error of at most 0.017.
Values may be sent and summed in bfloat16 or wider, within the bound.
No kernel may reach another device: no remote copies, remote signals or barrier semaphores. Data moves between devices by JAX's collectives and lax.ppermute only.
A program may use at most 64 MiB of HBM per device.

v0:
```python
import jax
import jax.numpy as jnp
from jax import lax
from jax.sharding import PartitionSpec as P

ROOT = 4096


def local(pressure, block_owner, level_one, level_one_map, level_two, level_two_map):
    members = lax.axis_size("se")
    member = lax.axis_index("se")
    block_count, cases, panel_rows = pressure.shape
    capacity = max(2, (2 * block_count + members - 1) // members)
    max_blocks = level_one.shape[2] // panel_rows
    half_dofs = level_two.shape[2]
    slot_count = members * capacity
    owner_table = lax.all_gather(block_owner, "se", axis=0, tiled=True)
    targets = jnp.arange(members, dtype=jnp.int32)
    table_hits = (owner_table[:, None] == targets[None, :]).astype(jnp.int32)
    dest_rank = jnp.sum(jnp.cumsum(table_hits, axis=0) * table_hits, axis=1) - 1
    source_hits = table_hits.reshape(members, block_count, members)
    local_rank = (jnp.sum(jnp.cumsum(source_hits, axis=1) * source_hits, axis=2) - 1).reshape(-1)
    sources = jnp.arange(members * block_count, dtype=jnp.int32) // block_count
    slots = jnp.arange(slot_count, dtype=jnp.int32)
    own_rank = lax.dynamic_slice_in_dim(local_rank, member * block_count, block_count)
    own_slot = block_owner * capacity + own_rank
    selector = (slots[:, None] == own_slot[None, :]).astype(jnp.bfloat16)
    outgoing = jnp.dot(
        selector,
        pressure.reshape(block_count, cases * panel_rows),
        preferred_element_type=jnp.float32,
    ).astype(jnp.bfloat16)
    incoming = lax.all_to_all(
        outgoing.reshape(members, capacity, cases, panel_rows),
        "se",
        split_axis=0,
        concat_axis=0,
        tiled=True,
    )
    arriving = owner_table == member
    rank_hits = (
        (dest_rank[:, None] == jnp.arange(max_blocks, dtype=jnp.int32)[None, :]) & arriving[:, None]
    ).astype(jnp.bfloat16)
    slot_hits = ((sources * capacity + local_rank)[:, None] == slots[None, :]).astype(jnp.bfloat16)
    placement = lax.dot_general(
        rank_hits, slot_hits, (((0,), (0,)), ((), ())), preferred_element_type=jnp.float32
    ).astype(jnp.bfloat16)
    interior = jnp.einsum(
        "kq,qcr->ckr",
        placement,
        incoming.reshape(slot_count, cases, panel_rows),
        preferred_element_type=jnp.float32,
    ).astype(jnp.bfloat16)
    interior = interior.reshape(cases, max_blocks * panel_rows)
    boundary = lax.dot_general(
        interior, level_one[0], (((1,), (1,)), ((), ())), preferred_element_type=jnp.float32
    )
    group_dofs = members * half_dofs
    term = jnp.zeros((cases, group_dofs), jnp.float32).at[:, level_one_map[0]].add(boundary)
    level_two_load = lax.psum_scatter(
        term.astype(jnp.bfloat16), "se", scatter_dimension=1, tiled=True
    ).astype(jnp.float32)
    loads = level_two_load.astype(jnp.bfloat16)
    partial_value = lax.dot_general(
        loads, level_two[0], (((1,), (1,)), ((), ())), preferred_element_type=jnp.float32
    )
    root_index = lax.dynamic_index_in_dim(level_two_map[0], member // 2, 0, keepdims=False)
    root_term = jnp.zeros((cases, ROOT), jnp.float32).at[:, root_index].add(partial_value)
    root_load = lax.psum_scatter(root_term, ("grp", "se"), scatter_dimension=1, tiled=True)
    return (level_two_load[None], root_load)


def solution(mesh):
    placed = (
        P(("grp", "se"), None, None),
        P(("grp", "se")),
        P(("grp", "se"), None, None),
        P(("grp", "se"), None),
        P("grp", None, "se"),
        P("grp", None, None),
    )
    return jax.shard_map(
        local,
        mesh=mesh,
        in_specs=placed,
        out_specs=(P("grp", None, "se"), P(None, ("grp", "se"))),
        check_vma=False,
    )
```

profile of v0, /device:TPU:1, one launch (start us, length us, event | category | flops | bytes accessed | tf_op | source)
XLA Modules:
  0.0 592.9 jit_solution(9521959657537069489)
XLA Ops:
  7.2 1.4 dynamic-slice.1
  9.3 0.9 dynamic-update-slice
  10.1 22.8 %all-reduce = s32[768]{0:T(1024)S(1)} all-reduce(s32[768]{0:T(1024)S(1)} %dynamic-update-slice), channel_id=1, replica_groups=mesh['grp'=16,'se'=32] {'se'}, use_global_device_ids=true, to_apply=%add | all-reduce | flops 768 | bytes 6144
  32.9 0.1 eq.78
  33.0 0.1 copy.18
  33.0 0.7 fusion.37
  33.8 0.1 copy.19
  33.8 0.1 sub.21
  33.9 0.7 dynamic-slice_add_fusion
  34.7 1.5 fusion.2
  36.1 1.3 copy.27
  37.5 4.7 all-to-all-start
  42.1 0.0 reduce-scatter.2.cloned.1.call-start
  42.2 1.7 reduce-window.6
  43.9 0.3 slice_reduce_fusion
  44.2 0.1 fusion.27
  44.4 16.9 %all-to-all-done = bf16[32,2,64,128]{3,2,1,0:T(8,128)(2,1)} async-done(((bf16[32,2,64,128]{3,2,1,0:T(8,128)(2,1)}), bf16[32,2,64,128]{3,2,1,0:T(8,128)(2,1)}, u32[]{:S(2)}, u32[]{:S(2)}) %all-to-all-start) | async-done | bytes 1048608 | tf_op jit(solution)/shard_map/all_to_all | solution.py:33
  61.3 3.3 copy.20
  64.6 3.0 convolution_convert_fusion.1
  67.6 2.2 fusion.3
  69.8 0.1 copy.22
  69.9 2.9 scatter_custom_fusion
  72.8 2.7 convert_element_type.34
  75.5 0.0 all-reduce.4.cloned.1.call-start
  75.6 0.7 fusion.36
  76.3 221.1 %reduce-scatter.2.cloned.1.call-done = bf16[64,128]{0,1:T(8,128)(2,1)} async-done(((bf16[64,4096]{0,1:T(8,128)(2,1)}), bf16[64,128]{0,1:T(8,128)(2,1)}) %reduce-scatter.2.cloned.1.call-update) | async-done | bytes 16400 | tf_op jit(solution)/shard_map/reduce_scatter | solution.py:60
  297.4 0.9 convolution_bitcast_fusion
  298.3 0.1 copy.23
  298.4 2.4 scatter_custom_fusion.1
  300.9 0.7 copy.24
  301.6 283.2 %all-reduce.4.cloned.1.call-done = f32[64,4096]{0,1:T(8,128)} async-done(((f32[64,4096]{0,1:T(8,128)}), f32[64,4096]{0,1:T(8,128)}) %all-reduce.4.cloned.1.call-update) | async-done | bytes 1048592
  584.8 1.3 constant_dynamic-slice_fusion
  (18 shorter events, 0.1 us)
Async XLA Ops:
  7.2 60.5 %copy-start = (bf16[1,256,6144]{2,1,0:T(8,128)(2,1)S(1)}, bf16[1,256,6144]{2,1,0:T(8,128)(2,1)}, u32[]{:S(2)}) copy-start(bf16[1,256,6144]{2,1,0:T(8,128)(2,1)} %param.8) | copy-start | bytes 9437188
  36.1 8.2 %copy-start.3 = (s32[1,256]{1,0:T(1,128)S(1)}, s32[1,256]{1,0:T(1,128)}, u32[]{:S(2)}) copy-start(s32[1,256]{1,0:T(1,128)} %param.9) | copy-start | bytes 3076
  37.5 23.8 %all-to-all-start = ((bf16[32,2,64,128]{3,2,1,0:T(8,128)(2,1)}), bf16[32,2,64,128]{3,2,1,0:T(8,128)(2,1)}, u32[]{:S(2)}, u32[]{:S(2)}) async-start(bf16[32,2,64,128]{3,2,1,0:T(8,128)(2,1)} %bitcast.60), calls=%async_computation | async-start | bytes 2097152 | tf_op jit(solution)/shard_map/all_to_all | solution.py:33
  42.1 255.2 %reduce-scatter.2.cloned.1.call-start = ((), (), s32[]{:S(2)}) async-start(), calls=%async_computation.2 | async-start | bytes 1081344 | tf_op jit(solution)/shard_map/reduce_scatter | solution.py:60
  72.8 224.6 %copy-start.2 = (bf16[1,128,128]{2,1,0:T(8,128)(2,1)S(1)}, bf16[1,128,128]{2,1,0:T(8,128)(2,1)}, u32[]{:S(2)}) copy-start(bf16[1,128,128]{2,1,0:T(8,128)(2,1)} %param.10) | copy-start | bytes 98308
  75.5 509.3 %all-reduce.4.cloned.1.call-start = ((), (), s32[]{:S(2)}) async-start(), calls=%async_computation.3 | async-start | bytes 4194304
  298.4 2.4 copy-start.1
Sparse Core Ops, SparseCore 0:
  75.6 221.6 reduce-scatter.1
  302.3 282.4 all-reduce.3
where the time goes:
time: 593 us
  waiting for transfers between devices  521 us (88%)
  blocking collectives  22.8 us (4%)
  between operations  14.9 us (3%)
  other arithmetic  12 us (2%)
  local copies, waits for them, and re-layouts  9.7 us (2%)
  matrix products  7.61 us (1%)
    unnamed x3, waiting for transfers between devices  283 us
    reduce_scatter x1, waiting for transfers between devices, local(): lax.psum_scatter(term.astype(jnp.bfloat16), 'se', scatter_dimension=1, ti...  221 us
    unnamed x1, blocking collectives  22.8 us
    all_to_all x1, waiting for transfers between devices, local(): lax.all_to_all(outgoing.reshape(members, capacity, cases, panel_rows), 's...  16.9 us
  transfers between devices with their start and end apart: 3, of which 3 were waited for; matrix products, arithmetic and copies ran while one was open for 1% of the time, Pallas kernels for 0%

commit v1 on v0

v1 whole, which is shorter than its diff:
```python
import jax
import jax.numpy as jnp
from jax import lax
from jax.experimental import pallas as pl
from jax.experimental.pallas import tpu as pltpu
from jax.sharding import PartitionSpec as P

ROOT = 4096
CAPACITY = 2
RC = 16
EMPTY = 64.0
BF16 = jnp.bfloat16
F32 = jnp.float32
I32 = jnp.int32
VMEM = pl.BlockSpec(memory_space=pltpu.VMEM)
SMEM = pl.BlockSpec(memory_space=pltpu.SMEM)
LIMIT = pltpu.CompilerParams(vmem_limit_bytes=24 * 1024 * 1024)


def iota(shape, dim):
    return lax.broadcasted_iota(I32, shape, dim)


def dot_nt(a, b):
    return lax.dot_general(a, b, (((1,), (1,)), ((), ())), preferred_element_type=F32)


def pack_kernel(owner_ref, pressure_ref, out_ref, count_ref):
    blocks = pressure_ref.shape[0]
    slots = out_ref.shape[0]
    members = slots // CAPACITY
    out_ref[:, 0:16, :] = jnp.full((slots, 16, out_ref.shape[2]), EMPTY, BF16)
    for e in range(members):
        count_ref[e] = 0
    for t in range(blocks):
        owner = owner_ref[t]
        count = count_ref[owner]
        count_ref[owner] = count + 1
        out_ref[owner * CAPACITY + count] = pressure_ref[t]


def pack(block_owner, pressure, members):
    _, cases, rows = pressure.shape
    return pl.pallas_call(
        pack_kernel,
        out_shape=jax.ShapeDtypeStruct((members * CAPACITY, cases, rows), BF16),
        in_specs=[SMEM, VMEM],
        out_specs=VMEM,
        scratch_shapes=[pltpu.SMEM((members,), I32)],
        compiler_params=LIMIT,
    )(block_owner, pressure)


def condense_kernel(incoming_ref, matrix_ref, slot_ref, offset_ref, out_ref, interior_ref, place_ref, place_smem, sem):
    slots, cases, rows = incoming_ref.shape
    most = matrix_ref.shape[1] // rows
    marks = incoming_ref[:, 0:16, :].astype(F32)[:, 0, 0:1]
    filled = (marks < EMPTY / 2).astype(F32)
    row, col = iota((slots, 128), 0), iota((slots, 128), 1)
    before = jnp.sum(jnp.where(row < col, filled, 0.0), axis=0, keepdims=True)
    here = jnp.sum(jnp.where(row == col, filled, 0.0), axis=0, keepdims=True)
    place = jnp.where(here > 0.5, before, float(most)).astype(I32)
    place_ref[...] = jnp.broadcast_to(place, place_ref.shape)
    copy = pltpu.make_async_copy(place_ref, place_smem, sem)
    copy.start()
    interior_ref[...] = jnp.zeros_like(interior_ref)
    copy.wait()
    for q in range(slots):
        at = pl.multiple_of(place_smem[0, q] * rows, rows)
        interior_ref[0:cases, pl.ds(at, rows)] = incoming_ref[q]
    boundary = dot_nt(matrix_ref[...], interior_ref[:, 0 : most * rows])
    lane = iota(boundary.shape, 1)
    with_offset = jnp.where(lane == cases, (offset_ref[...] + 1).astype(F32), boundary).astype(BF16)
    choose = (slot_ref[...] == iota((out_ref.shape[0], slot_ref.shape[1]), 0)).astype(F32).astype(BF16)
    out_ref[...] = jnp.dot(choose, with_offset, preferred_element_type=F32).astype(BF16)


def condense(incoming, matrix, slot, offset, members):
    slots, cases, rows = incoming.shape
    most = matrix.shape[1] // rows
    return pl.pallas_call(
        condense_kernel,
        out_shape=jax.ShapeDtypeStruct((members * RC, 128), BF16),
        in_specs=[VMEM] * 4,
        out_specs=VMEM,
        scratch_shapes=[
            pltpu.VMEM((128, (most + 1) * rows), BF16),
            pltpu.VMEM((8, 128), I32),
            pltpu.SMEM((8, 128), I32),
            pltpu.SemaphoreType.DMA,
        ],
        compiler_params=LIMIT,
    )(incoming, matrix, slot, offset)


def assemble_kernel(rows_ref, matrix_ref, root_ref, load_ref, out_ref):
    cases = load_ref.shape[0]
    groups = out_ref.shape[0]
    span = ROOT // groups
    rows = rows_ref[...]
    offsets = rows.astype(F32)[:, cases : cases + 1]
    hits = (offsets == (iota(rows.shape, 1) + 1).astype(F32)).astype(F32).astype(BF16)
    load = lax.dot_general(rows, hits, (((0,), (0,)), ((), ())), preferred_element_type=F32)[0:cases]
    load_ref[...] = load
    second = dot_nt(load.astype(BF16), matrix_ref[...]).astype(BF16)
    root = root_ref[...]
    for g in range(groups):
        out_ref[g, 0:cases, :] = second
        within = root - g * span
        index = jnp.where((within >= 0) & (within < span), within, 2 * span).astype(F32)
        out_ref[g, cases : cases + 16, :] = jnp.broadcast_to(index, (16, 128)).astype(BF16)


def assemble(rows, matrix, root, cases, groups):
    half = matrix.shape[1]
    return pl.pallas_call(
        assemble_kernel,
        out_shape=(
            jax.ShapeDtypeStruct((cases, half), F32),
            jax.ShapeDtypeStruct((groups, cases + 16, 128), BF16),
        ),
        in_specs=[VMEM] * 3,
        out_specs=(VMEM, VMEM),
        compiler_params=LIMIT,
    )(rows, matrix, root)


def root_kernel(parts_ref, out_ref):
    groups, depth, _ = parts_ref.shape
    cases = depth - 16
    span = out_ref.shape[0]
    want = iota((span, 128), 0).astype(F32)
    total = jnp.zeros(out_ref.shape, F32)
    for g in range(groups):
        index = parts_ref[g, cases : cases + 16, :].astype(F32)[0:1]
        hits = (want == index).astype(F32).astype(BF16)
        total += dot_nt(hits, parts_ref[g, 0:cases, :])
    out_ref[...] = total


def root_sum(parts, span, cases):
    return pl.pallas_call(
        root_kernel,
        out_shape=jax.ShapeDtypeStruct((span, cases), F32),
        in_specs=[VMEM],
        out_specs=VMEM,
        compiler_params=LIMIT,
    )(parts)


def exchange(x, axis):
    return lax.all_to_all(x, axis, split_axis=0, concat_axis=0, tiled=True)


def local(pressure, block_owner, level_one, level_one_map, level_two, level_two_map):
    members = lax.axis_size("se")
    groups = lax.axis_size("grp")
    member = lax.axis_index("se")
    cases, rows = pressure.shape[1:]
    half = level_two.shape[2]

    outgoing = pack(block_owner, pressure, members)
    incoming = exchange(outgoing, "se")

    target = level_one_map[0]
    dest = target // half
    dofs = jnp.arange(target.shape[0], dtype=I32)
    earlier = (dest[:, None] == dest[None, :]) & (dofs[:, None] < dofs[None, :])
    slot = dest * RC + jnp.sum(earlier.astype(I32), axis=0)
    offset = target - dest * half
    root = lax.dynamic_index_in_dim(level_two_map[0], member // 2, 0, keepdims=True)

    packed = condense(incoming, level_one[0], slot[None, :], offset[:, None], members)
    received = exchange(packed.reshape(members, RC, 128), "se").reshape(members * RC, 128)
    level_two_load, parts = assemble(received, level_two[0], root, cases, groups)
    parts = exchange(parts, "grp")
    span = ROOT // groups
    share = root_sum(parts, span, cases)
    share = exchange(share.reshape(members, span // members, cases), "se")
    root_load = jnp.sum(share, axis=0).T
    return (level_two_load[None], root_load)


def solution(mesh):
    placed = (
        P(("grp", "se"), None, None),
        P(("grp", "se")),
        P(("grp", "se"), None, None),
        P(("grp", "se"), None),
        P("grp", None, "se"),
        P("grp", None, None),
    )
    return jax.shard_map(
        local,
        mesh=mesh,
        in_specs=placed,
        out_specs=(P("grp", None, "se"), P(None, ("grp", "se"))),
        check_vma=False,
    )
```

time: 593 us -> 104 us (0.18)
  waiting for transfers between devices: 521 us -> 33.3 us
  starting transfers between devices: 4.74 us -> 22.4 us
  between operations: 14.9 us -> 0.77 us
  blocking collectives: 22.8 us -> 34.8 us
  other arithmetic: 12 us -> 1.67 us
  matrix products: 7.61 us -> 0 us
    unnamed x3 -> x0, waiting for transfers between devices: 283 us -> none
    reduce_scatter x1 -> x0, waiting for transfers between devices: 221 us -> none  [local(): lax.psum_scatter(term.astype(jnp.bfloat16), 'se', scatter_dimension=1, ti...]
    all_to_all x0 -> x2, blocking collectives: none -> 34.8 us  [exchange(): return lax.all_to_all(x, axis, split_axis=0, concat_axis=0, tiled=True)]
    unnamed x1 -> x0, blocking collectives: 22.8 us -> none
    all_to_all x1 -> x2, starting transfers between devices: 4.66 us -> 22.4 us  [exchange(): return lax.all_to_all(x, axis, split_axis=0, concat_axis=0, tiled=True)]
    all_to_all x1 -> x2, waiting for transfers between devices: 16.9 us -> 33.3 us  [exchange(): return lax.all_to_all(x, axis, split_axis=0, concat_axis=0, tiled=True)]
    dot_general x4 -> x0, matrix products: 7.61 us -> none  [the longest x1 3.03 us: local(): jnp.einsum('kq,qcr->ckr', placement, incoming.reshape(slot_count, cases,...]
  transfers between devices with their start and end apart: 3 -> 2, of which waited for: 3 -> 2; matrix products, arithmetic and copies ran while one was open for 1% -> 0% of each run, Pallas kernels for 0% -> 0%
where the time goes in v1:
time: 104 us; the launch traced here: 103 us
  blocking collectives  34.8 us (33%)
  waiting for transfers between devices  33.3 us (32%)
  starting transfers between devices  22.4 us (22%)
  Pallas kernels  5.87 us (6%)
  local copies, waits for them, and re-layouts  4.42 us (4%)
  other arithmetic  1.67 us (2%)
    all_to_all x2, blocking collectives, exchange(): return lax.all_to_all(x, axis, split_axis=0, concat_axis=0, tiled=True)  34.8 us
    all_to_all x2, waiting for transfers between devices, exchange(): return lax.all_to_all(x, axis, split_axis=0, concat_axis=0, tiled=True)  33.3 us
    all_to_all x2, starting transfers between devices, exchange(): return lax.all_to_all(x, axis, split_axis=0, concat_axis=0, tiled=True)  22.4 us
    unnamed x14, local copies, waits for them, and re-layouts  3.77 us
    pallas_call x1, Pallas kernels, condense(): pl.pallas_call(condense_kernel, out_shape=jax.ShapeDtypeStruct((members *...  2.95 us
  transfers between devices with their start and end apart: 2, of which 2 were waited for; matrix products, arithmetic and copies ran while one was open for 0% of the time, Pallas kernels for 0%

profile of v1, /device:TPU:1, one launch (start us, length us, event | category | flops | bytes accessed | tf_op | source)
XLA Modules:
  0.0 103.3 jit_solution(16209269591412541680)
XLA Ops:
  0.6 0.0 copy-start
  0.6 0.0 copy-start.2
  0.7 1.0 copy-done.2
  1.6 0.0 copy-start.4
  1.7 0.7 copy-done.4
  2.3 0.0 copy-start.5
  2.3 1.6 %shard_map.77 = bf16[64,64,128]{2,1,0:T(8,128)(2,1)} custom-call(s32[24]{0:T(128)S(1)} %copy-done.4, bf16[24,64,128]{2,1,0:T(8,128)(2,1)S(1)} %copy-done.2), custom_call_target="tpu_custom_call" | custom-call | tf_op jit(solution)/shard_map/pallas_call | solution.py:44
  3.9 0.0 copy-start.3
  3.9 13.8 %all-to-all-start = ((bf16[64,64,128]{2,1,0:T(8,128)(2,1)}), bf16[64,64,128]{2,1,0:T(8,128)(2,1)S(1)}, u32[]{:S(2)}, u32[]{:S(2)}) async-start(bf16[64,64,128]{2,1,0:T(8,128)(2,1)} %shard_map.77), calls=%async_computation | async-start | bytes 2097152 | tf_op jit(solution)/shard_map/all_to_all | solution.py:152
  17.8 0.0 copy-done.5
  17.8 0.1 copy.23
  18.0 0.1 convert_reduce_fusion
  18.1 0.1 fusion.3.offset_ref
  18.2 24.2 %all-to-all-done.incoming_ref = bf16[64,64,128]{2,1,0:T(8,128)(2,1)S(1)} async-done(((bf16[64,64,128]{2,1,0:T(8,128)(2,1)}), bf16[64,64,128]{2,1,0:T(8,128)(2,1)S(1)}, u32[]{:S(2)}, u32[]{:S(2)}) %all-to-all-start) | async-done | bytes 1048608 | tf_op jit(solution)/shard_map/all_to_all | solution.py:152
  42.4 0.0 copy-start.1
  42.4 1.9 %copy-done.1 = bf16[1,256,6144]{2,1,0:T(8,128)(2,1)S(1)} copy-done((bf16[1,256,6144]{2,1,0:T(8,128)(2,1)S(1)}, bf16[1,256,6144]{2,1,0:T(8,128)(2,1)}, u32[]{:S(2)}) %copy-start.1) | copy-done | bytes 3145752
  44.3 2.9 %shard_map.78 = bf16[512,128]{1,0:T(8,128)(2,1)} custom-call(bf16[64,64,128]{2,1,0:T(8,128)(2,1)S(1)} %all-to-all-done.incoming_ref, bf16[256,6144]{1,0:T(8,128)(2,1)S(1)} %bitcast.13, s32[1,256]{1,0:T(1,128)S(1)} %multiply_add_fusion.slot_ref, s32[256,1]{1,0:T(8,128)S(1)} %fusion.3.offset_ref), custom_call_target="tpu_custom_call" | custom-call | tf_op jit(solution)/shard_map/pallas_call | solution.py:81
  47.3 8.6 %all-to-all-start.1 = ((bf16[32,16,128]{2,1,0:T(8,128)(2,1)}), bf16[32,16,128]{2,1,0:T(8,128)(2,1)S(1)}, u32[]{:S(2)}, u32[]{:S(2)}) async-start(bf16[32,16,128]{2,1,0:T(8,128)(2,1)} %bitcast.5), calls=%async_computation.1 | async-start | bytes 262144 | tf_op jit(solution)/shard_map/all_to_all | solution.py:152
  55.9 0.0 copy-done
  55.9 9.1 %all-to-all-done.1 = bf16[32,16,128]{2,1,0:T(8,128)(2,1)S(1)} async-done(((bf16[32,16,128]{2,1,0:T(8,128)(2,1)}), bf16[32,16,128]{2,1,0:T(8,128)(2,1)S(1)}, u32[]{:S(2)}, u32[]{:S(2)}) %all-to-all-start.1) | async-done | bytes 131104 | tf_op jit(solution)/shard_map/all_to_all | solution.py:152
  65.0 0.0 copy-done.3
  65.0 0.9 shard_map.79
  65.9 22.7 %all_to_all.20.parts_ref = bf16[16,80,128]{2,1,0:T(8,128)(2,1)S(1)} all-to-all(bf16[16,80,128]{2,1,0:T(8,128)(2,1)S(1)} %get-tuple-element.5), channel_id=1, replica_groups=mesh['grp'=16,'se'=32] {'grp'}, dimensions={0} | all-to-all | bytes 655360 | tf_op jit(solution)/shard_map/all_to_all | solution.py:152
  88.6 0.4 shard_map.80
  89.0 0.1 reshape.109
  89.1 12.1 %all_to_all.21 = f32[32,1,512]{2,1,0:T(1,128)S(1)} all-to-all(f32[32,1,512]{2,1,0:T(1,128)S(1)} %reshape.109), channel_id=1, replica_groups=mesh['grp'=16,'se'=32] {'se'}, dimensions={0} | all-to-all | bytes 131072 | tf_op jit(solution)/shard_map/all_to_all | solution.py:152
  101.3 0.5 broadcast.104
  101.8 0.8 reduce
  102.6 0.1 reshape.110
  102.7 0.6 reduce_sum.22
  (4 shorter events, 0.0 us)
Async XLA Ops:
  0.6 55.3 %copy-start = (s32[1,16,128]{2,1,0:T(8,128)S(1)}, s32[1,16,128]{2,1,0:T(8,128)}, u32[]{:S(2)}) copy-start(s32[1,16,128]{2,1,0:T(8,128)} %param.11) | copy-start | bytes 24580
  0.6 1.0 copy-start.2
  1.6 0.7 copy-start.4
  2.3 15.5 %copy-start.5 = (s32[1,256]{1,0:T(1,128)S(1)}, s32[1,256]{1,0:T(1,128)}, u32[]{:S(2)}) copy-start(s32[1,256]{1,0:T(1,128)} %param.9) | copy-start | bytes 3076
  3.9 61.1 %copy-start.3 = (bf16[1,128,128]{2,1,0:T(8,128)(2,1)S(1)}, bf16[1,128,128]{2,1,0:T(8,128)(2,1)}, u32[]{:S(2)}) copy-start(bf16[1,128,128]{2,1,0:T(8,128)(2,1)} %param.10) | copy-start | bytes 98308
  3.9 38.5 %all-to-all-start = ((bf16[64,64,128]{2,1,0:T(8,128)(2,1)}), bf16[64,64,128]{2,1,0:T(8,128)(2,1)S(1)}, u32[]{:S(2)}, u32[]{:S(2)}) async-start(bf16[64,64,128]{2,1,0:T(8,128)(2,1)} %shard_map.77), calls=%async_computation | async-start | bytes 2097152 | tf_op jit(solution)/shard_map/all_to_all | solution.py:152
  42.4 1.9 %copy-start.1 = (bf16[1,256,6144]{2,1,0:T(8,128)(2,1)S(1)}, bf16[1,256,6144]{2,1,0:T(8,128)(2,1)}, u32[]{:S(2)}) copy-start(bf16[1,256,6144]{2,1,0:T(8,128)(2,1)} %param.8) | copy-start | bytes 9437188
  47.3 17.8 %all-to-all-start.1 = ((bf16[32,16,128]{2,1,0:T(8,128)(2,1)}), bf16[32,16,128]{2,1,0:T(8,128)(2,1)S(1)}, u32[]{:S(2)}, u32[]{:S(2)}) async-start(bf16[32,16,128]{2,1,0:T(8,128)(2,1)} %bitcast.5), calls=%async_computation.1 | async-start | bytes 262144 | tf_op jit(solution)/shard_map/all_to_all | solution.py:152

commit v2 on v1

v2 whole, which is shorter than its diff:
```python
import jax
import jax.numpy as jnp
from jax import lax
from jax.experimental import pallas as pl
from jax.experimental.pallas import tpu as pltpu
from jax.sharding import PartitionSpec as P

ROOT = 4096
CAPACITY = 2
RC = 16
LANES = 128
EMPTY = 64.0
BF16 = jnp.bfloat16
F32 = jnp.float32
I32 = jnp.int32
VMEM = pl.BlockSpec(memory_space=pltpu.VMEM)
SMEM = pl.BlockSpec(memory_space=pltpu.SMEM)
ANY = pl.BlockSpec(memory_space=pl.ANY)
LIMIT = pltpu.CompilerParams(vmem_limit_bytes=16 * 1024 * 1024)


def iota(shape, dim):
    return lax.broadcasted_iota(I32, shape, dim)


def dot_nt(a, b):
    return lax.dot_general(a, b, (((1,), (1,)), ((), ())), preferred_element_type=F32)


def dot_tn(a, b):
    return lax.dot_general(a, b, (((0,), (0,)), ((), ())), preferred_element_type=F32)


def one_hot(hits):
    return hits.astype(F32).astype(BF16)


def pack_kernel(owner_ref, pressure_ref, out_ref, owner_smem, count_ref, mark_ref, owner_sem, mark_sem, block_sem):
    blocks = pressure_ref.shape[0]
    slots = out_ref.shape[0]
    owners = pltpu.make_async_copy(owner_ref, owner_smem, owner_sem)
    owners.start()
    mark_ref[...] = jnp.full(mark_ref.shape, EMPTY, BF16)
    marks = pltpu.make_async_copy(mark_ref, out_ref.at[:, 0:16, :], mark_sem)
    marks.start()
    for e in range(slots // CAPACITY):
        count_ref[e] = 0
    owners.wait()
    marks.wait()
    copies = []
    for t in range(blocks):
        owner = owner_smem[t]
        count = count_ref[owner]
        count_ref[owner] = count + 1
        copy = pltpu.make_async_copy(pressure_ref.at[t], out_ref.at[owner * CAPACITY + count], block_sem.at[t])
        copy.start()
        copies.append(copy)
    for copy in copies:
        copy.wait()


def pack(block_owner, pressure, members):
    blocks, cases, rows = pressure.shape
    return pl.pallas_call(
        pack_kernel,
        out_shape=jax.ShapeDtypeStruct((members * CAPACITY, cases, rows), BF16),
        in_specs=[ANY, ANY],
        out_specs=ANY,
        scratch_shapes=[
            pltpu.SMEM((blocks,), I32),
            pltpu.SMEM((members,), I32),
            pltpu.VMEM((members * CAPACITY, 16, rows), BF16),
            pltpu.SemaphoreType.DMA,
            pltpu.SemaphoreType.DMA,
            pltpu.SemaphoreType.DMA((blocks,)),
        ],
        compiler_params=pltpu.CompilerParams(vmem_limit_bytes=60 * 1024 * 1024),
    )(block_owner, pressure)


def plan_kernel(target_ref, matrix_ref, out_ref):
    out_ref[...] = target_ref[...]


def plan(target, matrix):
    return pl.pallas_call(
        plan_kernel,
        out_shape=jax.ShapeDtypeStruct(target.shape, I32),
        in_specs=[VMEM, ANY],
        out_specs=VMEM,
        compiler_params=LIMIT,
    )(target, matrix)


def condense_kernel(
    arrived_ref, matrix_ref, slot_ref, target_ref, out_ref, incoming_ref, interior_ref, place_ref, place_smem, sem, in_sem
):
    slots, cases, rows = incoming_ref.shape
    most = matrix_ref.shape[1] // rows
    heads = pltpu.make_async_copy(arrived_ref.at[:, 0:16, :], incoming_ref.at[:, 0:16, :], in_sem.at[0])
    tails = pltpu.make_async_copy(arrived_ref.at[:, 16:cases, :], incoming_ref.at[:, 16:cases, :], in_sem.at[1])
    heads.start()
    tails.start()
    heads.wait()
    marks = incoming_ref[:, 0:16, :].astype(F32)[:, 0, 0:1]
    filled = (marks < EMPTY / 2).astype(F32)
    row, col = iota((slots, LANES), 0), iota((slots, LANES), 1)
    before = jnp.sum(jnp.where(row < col, filled, 0.0), axis=0, keepdims=True)
    here = jnp.sum(jnp.where(row == col, filled, 0.0), axis=0, keepdims=True)
    place = jnp.where(here > 0.5, before, float(most)).astype(I32)
    place_ref[...] = jnp.broadcast_to(place, place_ref.shape)
    copy = pltpu.make_async_copy(place_ref, place_smem, sem)
    copy.start()
    interior_ref[...] = jnp.zeros_like(interior_ref)
    copy.wait()
    tails.wait()
    for q in range(slots):
        at = pl.multiple_of(place_smem[0, q] * rows, rows)
        interior_ref[0:cases, pl.ds(at, rows)] = incoming_ref[q]
    boundary = dot_nt(matrix_ref[...], interior_ref[:, 0 : most * rows])
    parts = cases // 2
    lane = iota(boundary.shape, 1)
    dest = target_ref[...] // rows
    offset = (target_ref[...] - dest * rows + 1).astype(F32)
    own = jnp.where(lane == cases + parts, offset, jnp.where(lane < cases, boundary, 0.0))
    lower = pltpu.roll(boundary, cases, 1)
    upper = pltpu.roll(boundary, parts, 1)
    other = jnp.where(dest % 2 == 1, lower, upper)
    other = jnp.where((lane >= cases) & (lane < cases + parts), other, 0.0)
    other = jnp.where(lane == cases + parts + 1, offset, other)
    slot = slot_ref[...]
    want = iota((out_ref.shape[0], slot.shape[1]), 0)
    sent = jnp.dot(one_hot(slot == want), own.astype(BF16), preferred_element_type=F32)
    sent += jnp.dot(one_hot(slot == want ^ RC), other.astype(BF16), preferred_element_type=F32)
    out_ref[...] = sent.astype(BF16)


def condense(incoming, matrix, slot, target, members):
    slots, cases, rows = incoming.shape
    depth = matrix.shape[1]
    return pl.pallas_call(
        condense_kernel,
        out_shape=jax.ShapeDtypeStruct((members * RC, LANES), BF16),
        in_specs=[ANY, VMEM, VMEM, VMEM],
        out_specs=VMEM,
        scratch_shapes=[
            pltpu.VMEM(incoming.shape, BF16),
            pltpu.VMEM((LANES, depth + rows), BF16),
            pltpu.VMEM((8, LANES), I32),
            pltpu.SMEM((8, LANES), I32),
            pltpu.SemaphoreType.DMA,
            pltpu.SemaphoreType.DMA((2,)),
        ],
        compiler_params=LIMIT,
    )(incoming, matrix, slot, target)


def assemble_kernel(side_ref, rows_ref, matrix_ref, other_ref, root_ref, load_ref, out_ref):
    cases = load_ref.shape[0]
    parts = cases // 2
    groups = out_ref.shape[0]
    span = ROOT // groups
    rows = rows_ref[...]
    offsets = rows.astype(F32)[:, cases + parts : cases + parts + 2]
    want = (iota(rows.shape, 1) + 1).astype(F32)
    load = dot_tn(rows, one_hot(offsets[:, 0:1] == want))[0:cases]
    other = dot_tn(rows, one_hot(offsets[:, 1:2] == want))[cases : cases + parts]
    load_ref[...] = load
    second = dot_nt(load.astype(BF16), matrix_ref[...])
    second = jnp.where(side_ref[0] == 0, second[0:parts], second[parts:cases])
    second = (second + dot_nt(other.astype(BF16), other_ref[...])).astype(BF16)
    root = root_ref[...]
    for g in range(groups):
        out_ref[g, 0:parts, :] = second
        within = root - g * span
        index = jnp.where((within >= 0) & (within < span), within, 2 * span).astype(F32)
        out_ref[g, parts : parts + 8, :] = jnp.broadcast_to(index, (8, LANES)).astype(BF16)


def assemble(side, rows, matrix, other, root, cases, groups):
    half = matrix.shape[1]
    return pl.pallas_call(
        assemble_kernel,
        out_shape=(
            jax.ShapeDtypeStruct((cases, half), F32),
            jax.ShapeDtypeStruct((groups, cases // 2 + 8, LANES), BF16),
        ),
        in_specs=[SMEM, VMEM, VMEM, VMEM, VMEM],
        out_specs=(VMEM, VMEM),
        compiler_params=LIMIT,
    )(side, rows, matrix, other, root)


def root_kernel(side_ref, parts_ref, out_ref):
    groups, depth, _ = parts_ref.shape
    parts = depth - 8
    span = out_ref.shape[0]
    want = iota((span, LANES), 0).astype(F32)
    total = jnp.zeros((span, parts), F32)
    for g in range(groups):
        index = parts_ref[g, parts:depth, :].astype(F32)[0:1]
        total += dot_nt(one_hot(want == index), parts_ref[g, 0:parts, :])
    zero = jnp.zeros_like(total)
    first = side_ref[0] == 0
    out_ref[:, 0:parts] = jnp.where(first, total, zero)
    out_ref[:, parts : 2 * parts] = jnp.where(first, zero, total)
    out_ref[:, 2 * parts :] = jnp.zeros((span, LANES - 2 * parts), F32)


def root_sum(side, parts, span):
    return pl.pallas_call(
        root_kernel,
        out_shape=jax.ShapeDtypeStruct((span, LANES), F32),
        in_specs=[SMEM, VMEM],
        out_specs=VMEM,
        compiler_params=LIMIT,
    )(side, parts)


def last_kernel(shares_ref, out_ref):
    total = shares_ref[0]
    for s in range(1, shares_ref.shape[0]):
        total += shares_ref[s]
    out_ref[...] = total[:, 0 : out_ref.shape[1]]


def last_sum(shares, cases):
    return pl.pallas_call(
        last_kernel,
        out_shape=jax.ShapeDtypeStruct((shares.shape[1], cases), F32),
        in_specs=[VMEM],
        out_specs=VMEM,
        compiler_params=LIMIT,
    )(shares)


def exchange(x, axis):
    return lax.all_to_all(x, axis, split_axis=0, concat_axis=0, tiled=True)


def local(pressure, block_owner, level_one, level_one_map, level_two, level_two_map):
    members = lax.axis_size("se")
    groups = lax.axis_size("grp")
    member = lax.axis_index("se")
    cases = pressure.shape[1]
    half = level_two.shape[2]

    outgoing = pack(block_owner, pressure, members)
    incoming = exchange(outgoing, "se")

    target = plan(level_one_map, level_one[0])[0]
    dest = target // half
    dofs = jnp.arange(target.shape[0], dtype=I32)
    earlier = (dest[:, None] == dest[None, :]) & (dofs[:, None] < dofs[None, :])
    slot = dest * RC + jnp.sum(earlier.astype(I32), axis=0)
    root = lax.dynamic_index_in_dim(level_two_map[0], member // 2, 0, keepdims=True)
    side = (member % 2)[None]
    partner = lax.ppermute(level_two[0], "se", [(i, i ^ 1) for i in range(members)])
    target, partner = lax.optimization_barrier((target, partner))

    packed = condense(incoming, level_one[0], slot[None, :], target[:, None], members)
    received = exchange(packed.reshape(members, RC, LANES), "se").reshape(members * RC, LANES)
    level_two_load, parts = assemble(side, received, level_two[0], partner, root, cases, groups)
    parts = exchange(parts, "grp")
    span = ROOT // groups
    share = root_sum(side, parts, span)
    share = exchange(share.reshape(members, span // members, LANES), "se")
    root_load = last_sum(share, cases).T
    return (level_two_load[None], root_load)


def solution(mesh):
    placed = (
        P(("grp", "se"), None, None),
        P(("grp", "se")),
        P(("grp", "se"), None, None),
        P(("grp", "se"), None),
        P("grp", None, "se"),
        P("grp", None, None),
    )
    return jax.shard_map(
        local,
        mesh=mesh,
        in_specs=placed,
        out_specs=(P("grp", None, "se"), P(None, ("grp", "se"))),
        check_vma=False,
    )
```

time: 104 us -> 110 us (1.058)
  Pallas kernels: 5.87 us -> 20.2 us
  local copies, waits for them, and re-layouts: 4.42 us -> 0.16 us
  starting transfers between devices: 22.4 us -> 25.8 us
  blocking collectives: 34.8 us -> 31.7 us
  waiting for transfers between devices: 33.3 us -> 30.3 us
  other arithmetic: 1.67 us -> 0.15 us
    all_to_all x2, waiting for transfers between devices: 33.3 us -> 9.31 us  [exchange(): return lax.all_to_all(x, axis, split_axis=0, concat_axis=0, tiled=True)]
    ppermute x0 -> x1, waiting for transfers between devices: none -> 21 us  [local(): lax.ppermute(level_two[0], 'se', [(i, i ^ 1) for i in range(members)])]
    pallas_call x1, Pallas kernels: 1.63 us -> 14.1 us  [pack(): pl.pallas_call(pack_kernel, out_shape=jax.ShapeDtypeStruct((members * CAP...]
    unnamed x14 -> x8, local copies, waits for them, and re-layouts: 3.77 us -> 0.02 us
    ppermute x0 -> x1, starting transfers between devices: none -> 3.06 us  [local(): lax.ppermute(level_two[0], 'se', [(i, i ^ 1) for i in range(members)])]
    all_to_all x2, blocking collectives: 34.8 us -> 31.7 us  [exchange(): return lax.all_to_all(x, axis, split_axis=0, concat_axis=0, tiled=True)]
    pallas_call x1, Pallas kernels: 2.95 us -> 4.14 us  [condense(): pl.pallas_call(condense_kernel, out_shape=jax.ShapeDtypeStruct((members *...]
  transfers between devices with their start and end apart: 2 -> 3, of which waited for: 2 -> 3; matrix products, arithmetic and copies ran while one was open for 0% -> 0% of each run, Pallas kernels for 0% -> 0%
where the time goes in v2:
time: 110 us; the launch traced here: 109 us
  blocking collectives  31.7 us (29%)
  waiting for transfers between devices  30.3 us (28%)
  starting transfers between devices  25.8 us (23%)
  Pallas kernels  20.2 us (18%)
    all_to_all x2, blocking collectives, exchange(): return lax.all_to_all(x, axis, split_axis=0, concat_axis=0, tiled=True)  31.7 us
    all_to_all x2, starting transfers between devices, exchange(): return lax.all_to_all(x, axis, split_axis=0, concat_axis=0, tiled=True)  22.7 us
    ppermute x1, waiting for transfers between devices, local(): lax.ppermute(level_two[0], 'se', [(i, i ^ 1) for i in range(members)])  21 us
    pallas_call x1, Pallas kernels, pack(): pl.pallas_call(pack_kernel, out_shape=jax.ShapeDtypeStruct((members * CAP...  14.1 us
    all_to_all x2, waiting for transfers between devices, exchange(): return lax.all_to_all(x, axis, split_axis=0, concat_axis=0, tiled=True)  9.31 us
    pallas_call x1, Pallas kernels, condense(): pl.pallas_call(condense_kernel, out_shape=jax.ShapeDtypeStruct((members *...  4.14 us
    ppermute x1, starting transfers between devices, local(): lax.ppermute(level_two[0], 'se', [(i, i ^ 1) for i in range(members)])  3.06 us
  transfers between devices with their start and end apart: 3, of which 3 were waited for; matrix products, arithmetic and copies ran while one was open for 0% of the time, Pallas kernels for 0%

profile of v2, /device:TPU:1, one launch (start us, length us, event | category | flops | bytes accessed | tf_op | source)
XLA Modules:
  0.0 109.2 jit_solution(10493441965121914099)
XLA Ops:
  0.6 0.0 copy-start
  0.6 0.0 copy-start.2
  0.7 0.0 copy-start.1
  0.7 0.0 copy-start.3
  0.7 14.1 %shard_map.77 = bf16[64,64,128]{2,1,0:T(8,128)(2,1)} custom-call(s32[24]{0:T(128)} %owner_ref.1, bf16[24,64,128]{2,1,0:T(8,128)(2,1)} %pressure_ref.1), custom_call_target="tpu_custom_call" | custom-call | tf_op jit(solution)/shard_map/pallas_call | solution.py:64
  14.7 13.9 %all-to-all-start = ((bf16[64,64,128]{2,1,0:T(8,128)(2,1)}), bf16[64,64,128]{2,1,0:T(8,128)(2,1)}, u32[]{:S(2)}, u32[]{:S(2)}) async-start(bf16[64,64,128]{2,1,0:T(8,128)(2,1)} %shard_map.77), calls=%async_computation | async-start | bytes 2097152 | tf_op jit(solution)/shard_map/all_to_all | solution.py:238
  28.6 0.0 copy-done.2
  28.6 3.1 %collective-permute-start = (bf16[128,128]{1,0:T(8,128)(2,1)S(1)}, bf16[128,128]{1,0:T(8,128)(2,1)S(1)}, u32[]{:S(2)}, u32[]{:S(2)}) collective-permute-start(bf16[128,128]{1,0:T(8,128)(2,1)S(1)} %bitcast.18), channel_id=1, source_target_pairs={{0,1},{1,0},{2,3},{3,2},{4,5},{5,4},{6,7},{7,6},{8,9},{9,8},{10,11... | collective-permute-start | bytes 98312 | tf_op jit(solution)/shard_map/ppermute | solution.py:258
  31.7 0.0 copy-done.1
  31.7 0.0 copy-done.3
  31.8 0.1 convert_reduce_fusion
  31.9 21.0 %collective-permute-done.other_ref = bf16[128,128]{1,0:T(8,128)(2,1)S(1)} collective-permute-done((bf16[128,128]{1,0:T(8,128)(2,1)S(1)}, bf16[128,128]{1,0:T(8,128)(2,1)S(1)}, u32[]{:S(2)}, u32[]{:S(2)}) %collective-permute-start) | collective-permute-done | bytes 32800 | tf_op jit(solution)/shard_map/ppermute | solution.py:258
  52.9 0.1 copy.9.target_ref
  53.0 0.2 all-to-all-done.arrived_ref
  53.2 4.1 %shard_map.79 = bf16[512,128]{1,0:T(8,128)(2,1)} custom-call(bf16[64,64,128]{2,1,0:T(8,128)(2,1)} %all-to-all-done.arrived_ref, bf16[256,6144]{1,0:T(8,128)(2,1)S(1)} %bitcast.15, s32[1,256]{1,0:T(1,128)S(1)} %multiply_add_fusion.slot_ref, s32[256,1]{1,0:T(8,128)S(1)} %copy.9.target_ref), custom_call_target="tpu_custom_call" | custom-call | tf_op jit(solution)/shard_map/pallas_call | solution.py:141
  57.4 8.9 %all-to-all-start.1 = ((bf16[32,16,128]{2,1,0:T(8,128)(2,1)}), bf16[32,16,128]{2,1,0:T(8,128)(2,1)S(1)}, u32[]{:S(2)}, u32[]{:S(2)}) async-start(bf16[32,16,128]{2,1,0:T(8,128)(2,1)} %bitcast.7), calls=%async_computation.1 | async-start | bytes 262144 | tf_op jit(solution)/shard_map/all_to_all | solution.py:238
  66.3 0.0 copy-done
  66.3 9.1 %all-to-all-done.1 = bf16[32,16,128]{2,1,0:T(8,128)(2,1)S(1)} async-done(((bf16[32,16,128]{2,1,0:T(8,128)(2,1)}), bf16[32,16,128]{2,1,0:T(8,128)(2,1)S(1)}, u32[]{:S(2)}, u32[]{:S(2)}) %all-to-all-start.1) | async-done | bytes 131104 | tf_op jit(solution)/shard_map/all_to_all | solution.py:238
  75.4 0.9 shard_map.80
  76.3 19.3 %all_to_all.20.parts_ref = bf16[16,40,128]{2,1,0:T(8,128)(2,1)S(1)} all-to-all(bf16[16,40,128]{2,1,0:T(8,128)(2,1)S(1)} %get-tuple-element.9), channel_id=1, replica_groups=mesh['grp'=16,'se'=32] {'grp'}, dimensions={0} | all-to-all | bytes 327680 | tf_op jit(solution)/shard_map/all_to_all | solution.py:238
  95.7 0.5 shard_map.81
  96.1 12.4 %all_to_all.21.shares_ref = f32[32,8,128]{2,1,0:T(8,128)S(1)} all-to-all(f32[32,8,128]{2,1,0:T(8,128)S(1)} %bitcast.17), channel_id=1, replica_groups=mesh['grp'=16,'se'=32] {'se'}, dimensions={0} | all-to-all | bytes 262144 | tf_op jit(solution)/shard_map/all_to_all | solution.py:238
  108.6 0.6 shard_map.82
  (5 shorter events, 0.0 us)
Async XLA Ops:
  0.6 65.7 %copy-start = (s32[1,16,128]{2,1,0:T(8,128)S(1)}, s32[1,16,128]{2,1,0:T(8,128)}, u32[]{:S(2)}) copy-start(s32[1,16,128]{2,1,0:T(8,128)} %param.11) | copy-start | bytes 24580
  0.6 28.0 %copy-start.2 = (bf16[1,128,128]{2,1,0:T(8,128)(2,1)S(1)}, bf16[1,128,128]{2,1,0:T(8,128)(2,1)}, u32[]{:S(2)}) copy-start(bf16[1,128,128]{2,1,0:T(8,128)(2,1)} %param.10) | copy-start | bytes 98308
  0.7 31.0 %copy-start.1 = (bf16[1,256,6144]{2,1,0:T(8,128)(2,1)S(1)}, bf16[1,256,6144]{2,1,0:T(8,128)(2,1)}, u32[]{:S(2)}) copy-start(bf16[1,256,6144]{2,1,0:T(8,128)(2,1)} %param.8) | copy-start | bytes 9437188
  0.7 31.0 %copy-start.3 = (s32[1,256]{1,0:T(1,128)S(1)}, s32[1,256]{1,0:T(1,128)}, u32[]{:S(2)}) copy-start(s32[1,256]{1,0:T(1,128)} %target_ref.1) | copy-start | bytes 3076
  14.7 38.5 %all-to-all-start = ((bf16[64,64,128]{2,1,0:T(8,128)(2,1)}), bf16[64,64,128]{2,1,0:T(8,128)(2,1)}, u32[]{:S(2)}, u32[]{:S(2)}) async-start(bf16[64,64,128]{2,1,0:T(8,128)(2,1)} %shard_map.77), calls=%async_computation | async-start | bytes 2097152 | tf_op jit(solution)/shard_map/all_to_all | solution.py:238
  28.6 24.3 %collective-permute-start = (bf16[128,128]{1,0:T(8,128)(2,1)S(1)}, bf16[128,128]{1,0:T(8,128)(2,1)S(1)}, u32[]{:S(2)}, u32[]{:S(2)}) collective-permute-start(bf16[128,128]{1,0:T(8,128)(2,1)S(1)} %bitcast.18), channel_id=1, source_target_pairs={{0,1},{1,0},{2,3},{3,2},{4,5},{5,4},{6,7},{7,6},{8,9},{9,8},{10,11... | collective-permute-start | bytes 98312 | tf_op jit(solution)/shard_map/ppermute | solution.py:258
  57.4 18.1 %all-to-all-start.1 = ((bf16[32,16,128]{2,1,0:T(8,128)(2,1)}), bf16[32,16,128]{2,1,0:T(8,128)(2,1)S(1)}, u32[]{:S(2)}, u32[]{:S(2)}) async-start(bf16[32,16,128]{2,1,0:T(8,128)(2,1)} %bitcast.7), calls=%async_computation.1 | async-start | bytes 262144 | tf_op jit(solution)/shard_map/all_to_all | solution.py:238

commit v3 on v2

--- a/solution.py
+++ b/solution.py
@@ -9,6 +9,7 @@
 CAPACITY = 2
 RC = 16
 LANES = 128
+CHUNKS = 4
 EMPTY = 64.0
 BF16 = jnp.bfloat16
 F32 = jnp.float32
@@ -16,6 +17,8 @@
 VMEM = pl.BlockSpec(memory_space=pltpu.VMEM)
 SMEM = pl.BlockSpec(memory_space=pltpu.SMEM)
 ANY = pl.BlockSpec(memory_space=pl.ANY)
+WIDE = pltpu.CompilerParams(vmem_limit_bytes=62 * 1024 * 1024)
+ROOMY = pltpu.CompilerParams(vmem_limit_bytes=52 * 1024 * 1024)
 LIMIT = pltpu.CompilerParams(vmem_limit_bytes=16 * 1024 * 1024)
 
 
@@ -35,28 +38,22 @@
     return hits.astype(F32).astype(BF16)
 
 
-def pack_kernel(owner_ref, pressure_ref, out_ref, owner_smem, count_ref, mark_ref, owner_sem, mark_sem, block_sem):
-    blocks = pressure_ref.shape[0]
+def pack_kernel(owner_ref, pressure_ref, out_ref, held_ref, owner_smem, count_ref, owner_sem, block_sem):
     slots = out_ref.shape[0]
     owners = pltpu.make_async_copy(owner_ref, owner_smem, owner_sem)
+    blocks = pltpu.make_async_copy(pressure_ref, held_ref, block_sem)
     owners.start()
-    mark_ref[...] = jnp.full(mark_ref.shape, EMPTY, BF16)
-    marks = pltpu.make_async_copy(mark_ref, out_ref.at[:, 0:16, :], mark_sem)
-    marks.start()
+    blocks.start()
+    out_ref[:, 0:16, :] = jnp.full((slots, 16, out_ref.shape[2]), EMPTY, BF16)
     for e in range(slots // CAPACITY):
         count_ref[e] = 0
     owners.wait()
-    marks.wait()
-    copies = []
-    for t in range(blocks):
+    blocks.wait()
+    for t in range(held_ref.shape[0]):
         owner = owner_smem[t]
         count = count_ref[owner]
         count_ref[owner] = count + 1
-        copy = pltpu.make_async_copy(pressure_ref.at[t], out_ref.at[owner * CAPACITY + count], block_sem.at[t])
-        copy.start()
-        copies.append(copy)
-    for copy in copies:
-        copy.wait()
+        out_ref[owner * CAPACITY + count] = held_ref[t]
 
 
 def pack(block_owner, pressure, members):
@@ -65,59 +62,44 @@
         pack_kernel,
         out_shape=jax.ShapeDtypeStruct((members * CAPACITY, cases, rows), BF16),
         in_specs=[ANY, ANY],
-        out_specs=ANY,
+        out_specs=VMEM,
         scratch_shapes=[
+            pltpu.VMEM((blocks, cases, rows), BF16),
             pltpu.SMEM((blocks,), I32),
             pltpu.SMEM((members,), I32),
-            pltpu.VMEM((members * CAPACITY, 16, rows), BF16),
             pltpu.SemaphoreType.DMA,
             pltpu.SemaphoreType.DMA,
-            pltpu.SemaphoreType.DMA((blocks,)),
         ],
-        compiler_params=pltpu.CompilerParams(vmem_limit_bytes=60 * 1024 * 1024),
+        compiler_params=WIDE,
     )(block_owner, pressure)
 
 
-def plan_kernel(target_ref, matrix_ref, out_ref):
-    out_ref[...] = target_ref[...]
-
-
-def plan(target, matrix):
-    return pl.pallas_call(
-        plan_kernel,
-        out_shape=jax.ShapeDtypeStruct(target.shape, I32),
-        in_specs=[VMEM, ANY],
-        out_specs=VMEM,
-        compiler_params=LIMIT,
-    )(target, matrix)
-
-
 def condense_kernel(
-    arrived_ref, matrix_ref, slot_ref, target_ref, out_ref, incoming_ref, interior_ref, place_ref, place_smem, sem, in_sem
+    incoming_ref, level_ref, slot_ref, target_ref, out_ref, matrix_ref, interior_ref, level_sem
 ):
     slots, cases, rows = incoming_ref.shape
     most = matrix_ref.shape[1] // rows
-    heads = pltpu.make_async_copy(arrived_ref.at[:, 0:16, :], incoming_ref.at[:, 0:16, :], in_sem.at[0])
-    tails = pltpu.make_async_copy(arrived_ref.at[:, 16:cases, :], incoming_ref.at[:, 16:cases, :], in_sem.at[1])
-    heads.start()
-    tails.start()
-    heads.wait()
+    width = most * rows // CHUNKS
+    chunks = []
+    for c in range(CHUNKS):
+        part = (slice(None), slice(c * width, (c + 1) * width))
+        chunks.append(pltpu.make_async_copy(level_ref.at[part], matrix_ref.at[part], level_sem.at[c]))
+        chunks[c].start()
+    interior_ref[...] = jnp.zeros_like(interior_ref)
     marks = incoming_ref[:, 0:16, :].astype(F32)[:, 0, 0:1]
     filled = (marks < EMPTY / 2).astype(F32)
     row, col = iota((slots, LANES), 0), iota((slots, LANES), 1)
     before = jnp.sum(jnp.where(row < col, filled, 0.0), axis=0, keepdims=True)
     here = jnp.sum(jnp.where(row == col, filled, 0.0), axis=0, keepdims=True)
-    place = jnp.where(here > 0.5, before, float(most)).astype(I32)
-    place_ref[...] = jnp.broadcast_to(place, place_ref.shape)
-    copy = pltpu.make_async_copy(place_ref, place_smem, sem)
-    copy.start()
-    interior_ref[...] = jnp.zeros_like(interior_ref)
-    copy.wait()
-    tails.wait()
+    place = jnp.where(here > 0.5, before, float(most)).astype(I32) * rows
     for q in range(slots):
-        at = pl.multiple_of(place_smem[0, q] * rows, rows)
+        at = pl.multiple_of(place[0, q], rows)
         interior_ref[0:cases, pl.ds(at, rows)] = incoming_ref[q]
-    boundary = dot_nt(matrix_ref[...], interior_ref[:, 0 : most * rows])
+    boundary = jnp.zeros((matrix_ref.shape[0], LANES), F32)
+    for c in range(CHUNKS):
+        chunks[c].wait()
+        span = slice(c * width, (c + 1) * width)
+        boundary += dot_nt(matrix_ref[:, span], interior_ref[:, span])
     parts = cases // 2
     lane = iota(boundary.shape, 1)
     dest = target_ref[...] // rows
@@ -136,22 +118,19 @@
 
 
 def condense(incoming, matrix, slot, target, members):
-    slots, cases, rows = incoming.shape
     depth = matrix.shape[1]
+    rows = incoming.shape[2]
     return pl.pallas_call(
         condense_kernel,
         out_shape=jax.ShapeDtypeStruct((members * RC, LANES), BF16),
-        in_specs=[ANY, VMEM, VMEM, VMEM],
+        in_specs=[VMEM, ANY, VMEM, VMEM],
         out_specs=VMEM,
         scratch_shapes=[
-            pltpu.VMEM(incoming.shape, BF16),
+            pltpu.VMEM(matrix.shape, BF16),
             pltpu.VMEM((LANES, depth + rows), BF16),
-            pltpu.VMEM((8, LANES), I32),
-            pltpu.SMEM((8, LANES), I32),
-            pltpu.SemaphoreType.DMA,
-            pltpu.SemaphoreType.DMA((2,)),
+            pltpu.SemaphoreType.DMA((CHUNKS,)),
         ],
-        compiler_params=LIMIT,
+        compiler_params=ROOMY,
     )(incoming, matrix, slot, target)
 
 
@@ -248,7 +227,7 @@
     outgoing = pack(block_owner, pressure, members)
     incoming = exchange(outgoing, "se")
 
-    target = plan(level_one_map, level_one[0])[0]
+    target = level_one_map[0]
     dest = target // half
     dofs = jnp.arange(target.shape[0], dtype=I32)
     earlier = (dest[:, None] == dest[None, :]) & (dofs[:, None] < dofs[None, :])

time: 110 us -> 98.2 us (0.89)
  Pallas kernels: 20.2 us -> 8.92 us
    pallas_call x1, Pallas kernels: 14.1 us -> 2.1 us  [pack(): pl.pallas_call(pack_kernel, out_shape=jax.ShapeDtypeStruct((members * CAP...]
where the time goes in v3:
time: 98.2 us; the launch traced here: 97.8 us
  blocking collectives  31.8 us (32%)
  waiting for transfers between devices  30.3 us (31%)
  starting transfers between devices  25.8 us (26%)
  Pallas kernels  8.92 us (9%)
    all_to_all x2, blocking collectives, exchange(): return lax.all_to_all(x, axis, split_axis=0, concat_axis=0, tiled=True)  31.8 us
    all_to_all x2, starting transfers between devices, exchange(): return lax.all_to_all(x, axis, split_axis=0, concat_axis=0, tiled=True)  22.6 us
    ppermute x1, waiting for transfers between devices, local(): lax.ppermute(level_two[0], 'se', [(i, i ^ 1) for i in range(members)])  21 us
    all_to_all x2, waiting for transfers between devices, exchange(): return lax.all_to_all(x, axis, split_axis=0, concat_axis=0, tiled=True)  9.31 us
    pallas_call x1, Pallas kernels, condense(): pl.pallas_call(condense_kernel, out_shape=jax.ShapeDtypeStruct((members *...  4.82 us
    ppermute x1, starting transfers between devices, local(): lax.ppermute(level_two[0], 'se', [(i, i ^ 1) for i in range(members)])  3.14 us
    pallas_call x1, Pallas kernels, pack(): pl.pallas_call(pack_kernel, out_shape=jax.ShapeDtypeStruct((members * CAP...  2.1 us
  transfers between devices with their start and end apart: 3, of which 3 were waited for; matrix products, arithmetic and copies ran while one was open for 0% of the time, Pallas kernels for 0%

profile of v3, /device:TPU:1, one launch (start us, length us, event | category | flops | bytes accessed | tf_op | source)
XLA Modules:
  0.0 97.8 jit_solution(3929771936912890114)
XLA Ops:
  0.6 0.0 copy-start
  0.6 0.0 copy-start.1
  0.7 0.0 copy-start.2
  0.7 2.1 %shard_map.77 = bf16[64,64,128]{2,1,0:T(8,128)(2,1)} custom-call(s32[24]{0:T(128)} %owner_ref.1, bf16[24,64,128]{2,1,0:T(8,128)(2,1)} %pressure_ref.1), custom_call_target="tpu_custom_call" | custom-call | tf_op jit(solution)/shard_map/pallas_call | solution.py:61
  2.8 13.7 %all-to-all-start = ((bf16[64,64,128]{2,1,0:T(8,128)(2,1)}), bf16[64,64,128]{2,1,0:T(8,128)(2,1)S(1)}, u32[]{:S(2)}, u32[]{:S(2)}) async-start(bf16[64,64,128]{2,1,0:T(8,128)(2,1)} %shard_map.77), calls=%async_computation | async-start | bytes 2097152 | tf_op jit(solution)/shard_map/all_to_all | solution.py:217
  16.5 0.0 copy-done.1
  16.5 3.1 %collective-permute-start = (bf16[128,128]{1,0:T(8,128)(2,1)S(1)}, bf16[128,128]{1,0:T(8,128)(2,1)S(1)}, u32[]{:S(2)}, u32[]{:S(2)}) collective-permute-start(bf16[128,128]{1,0:T(8,128)(2,1)S(1)} %bitcast.16), channel_id=1, source_target_pairs={{0,1},{1,0},{2,3},{3,2},{4,5},{5,4},{6,7},{7,6},{8,9},{9,8},{10,11... | collective-permute-start | bytes 98312 | tf_op jit(solution)/shard_map/ppermute | solution.py:237
  19.7 0.0 copy-done.2
  19.7 0.1 convert_reduce_fusion
  19.8 21.0 %collective-permute-done.other_ref = bf16[128,128]{1,0:T(8,128)(2,1)S(1)} collective-permute-done((bf16[128,128]{1,0:T(8,128)(2,1)S(1)}, bf16[128,128]{1,0:T(8,128)(2,1)S(1)}, u32[]{:S(2)}, u32[]{:S(2)}) %collective-permute-start) | collective-permute-done | bytes 32800 | tf_op jit(solution)/shard_map/ppermute | solution.py:237
  40.8 0.1 copy.9.target_ref
  41.0 0.2 all-to-all-done.incoming_ref
  41.1 4.8 %shard_map.78 = bf16[512,128]{1,0:T(8,128)(2,1)} custom-call(bf16[64,64,128]{2,1,0:T(8,128)(2,1)S(1)} %all-to-all-done.incoming_ref, bf16[256,6144]{1,0:T(8,128)(2,1)} %bitcast.18, s32[1,256]{1,0:T(1,128)S(1)} %multiply_add_fusion.slot_ref, s32[256,1]{1,0:T(8,128)S(1)} %copy.9.target_ref), custom_call_target="tpu_custom_call" | custom-call | tf_op jit(solution)/shard_map/pallas_call | solution.py:123
  46.0 8.9 %all-to-all-start.1 = ((bf16[32,16,128]{2,1,0:T(8,128)(2,1)}), bf16[32,16,128]{2,1,0:T(8,128)(2,1)S(1)}, u32[]{:S(2)}, u32[]{:S(2)}) async-start(bf16[32,16,128]{2,1,0:T(8,128)(2,1)} %bitcast.7), calls=%async_computation.1 | async-start | bytes 262144 | tf_op jit(solution)/shard_map/all_to_all | solution.py:217
  54.9 0.0 copy-done
  54.9 9.1 %all-to-all-done.1 = bf16[32,16,128]{2,1,0:T(8,128)(2,1)S(1)} async-done(((bf16[32,16,128]{2,1,0:T(8,128)(2,1)}), bf16[32,16,128]{2,1,0:T(8,128)(2,1)S(1)}, u32[]{:S(2)}, u32[]{:S(2)}) %all-to-all-start.1) | async-done | bytes 131104 | tf_op jit(solution)/shard_map/all_to_all | solution.py:217
  64.0 0.9 shard_map.79
  64.9 19.3 %all_to_all.20.parts_ref = bf16[16,40,128]{2,1,0:T(8,128)(2,1)S(1)} all-to-all(bf16[16,40,128]{2,1,0:T(8,128)(2,1)S(1)} %get-tuple-element.9), channel_id=1, replica_groups=mesh['grp'=16,'se'=32] {'grp'}, dimensions={0} | all-to-all | bytes 327680 | tf_op jit(solution)/shard_map/all_to_all | solution.py:217
  84.3 0.5 shard_map.80
  84.7 12.5 %all_to_all.21.shares_ref = f32[32,8,128]{2,1,0:T(8,128)S(1)} all-to-all(f32[32,8,128]{2,1,0:T(8,128)S(1)} %bitcast.15), channel_id=1, replica_groups=mesh['grp'=16,'se'=32] {'se'}, dimensions={0} | all-to-all | bytes 262144 | tf_op jit(solution)/shard_map/all_to_all | solution.py:217
  97.2 0.6 shard_map.81
  (4 shorter events, 0.0 us)
Async XLA Ops:
  0.6 54.2 %copy-start = (s32[1,16,128]{2,1,0:T(8,128)S(1)}, s32[1,16,128]{2,1,0:T(8,128)}, u32[]{:S(2)}) copy-start(s32[1,16,128]{2,1,0:T(8,128)} %param.11) | copy-start | bytes 24580
  0.6 15.9 %copy-start.1 = (bf16[1,128,128]{2,1,0:T(8,128)(2,1)S(1)}, bf16[1,128,128]{2,1,0:T(8,128)(2,1)}, u32[]{:S(2)}) copy-start(bf16[1,128,128]{2,1,0:T(8,128)(2,1)} %param.10) | copy-start | bytes 98308
  0.7 19.0 %copy-start.2 = (s32[1,256]{1,0:T(1,128)S(1)}, s32[1,256]{1,0:T(1,128)}, u32[]{:S(2)}) copy-start(s32[1,256]{1,0:T(1,128)} %param.9) | copy-start | bytes 3076
  2.8 38.4 %all-to-all-start = ((bf16[64,64,128]{2,1,0:T(8,128)(2,1)}), bf16[64,64,128]{2,1,0:T(8,128)(2,1)S(1)}, u32[]{:S(2)}, u32[]{:S(2)}) async-start(bf16[64,64,128]{2,1,0:T(8,128)(2,1)} %shard_map.77), calls=%async_computation | async-start | bytes 2097152 | tf_op jit(solution)/shard_map/all_to_all | solution.py:217
  16.5 24.3 %collective-permute-start = (bf16[128,128]{1,0:T(8,128)(2,1)S(1)}, bf16[128,128]{1,0:T(8,128)(2,1)S(1)}, u32[]{:S(2)}, u32[]{:S(2)}) collective-permute-start(bf16[128,128]{1,0:T(8,128)(2,1)S(1)} %bitcast.16), channel_id=1, source_target_pairs={{0,1},{1,0},{2,3},{3,2},{4,5},{5,4},{6,7},{7,6},{8,9},{9,8},{10,11... | collective-permute-start | bytes 98312 | tf_op jit(solution)/shard_map/ppermute | solution.py:237
  46.0 18.1 %all-to-all-start.1 = ((bf16[32,16,128]{2,1,0:T(8,128)(2,1)}), bf16[32,16,128]{2,1,0:T(8,128)(2,1)S(1)}, u32[]{:S(2)}, u32[]{:S(2)}) async-start(bf16[32,16,128]{2,1,0:T(8,128)(2,1)} %bitcast.7), calls=%async_computation.1 | async-start | bytes 262144 | tf_op jit(solution)/shard_map/all_to_all | solution.py:217

commit v4 on v3

--- a/solution.py
+++ b/solution.py
@@ -9,7 +9,6 @@
 CAPACITY = 2
 RC = 16
 LANES = 128
-CHUNKS = 4
 EMPTY = 64.0
 BF16 = jnp.bfloat16
 F32 = jnp.float32
@@ -17,8 +16,8 @@
 VMEM = pl.BlockSpec(memory_space=pltpu.VMEM)
 SMEM = pl.BlockSpec(memory_space=pltpu.SMEM)
 ANY = pl.BlockSpec(memory_space=pl.ANY)
-WIDE = pltpu.CompilerParams(vmem_limit_bytes=62 * 1024 * 1024)
-ROOMY = pltpu.CompilerParams(vmem_limit_bytes=52 * 1024 * 1024)
+WIDE = pltpu.CompilerParams(vmem_limit_bytes=60 * 1024 * 1024)
+ROOMY = pltpu.CompilerParams(vmem_limit_bytes=16 * 1024 * 1024)
 LIMIT = pltpu.CompilerParams(vmem_limit_bytes=16 * 1024 * 1024)
 
 
@@ -74,18 +73,29 @@
     )(block_owner, pressure)
 
 
+def plan_kernel(target_ref, matrix_ref, out_ref):
+    out_ref[...] = target_ref[...]
+
+
+def plan(target, matrix):
+    return pl.pallas_call(
+        plan_kernel,
+        out_shape=jax.ShapeDtypeStruct(target.shape, I32),
+        in_specs=[VMEM, ANY],
+        out_specs=VMEM,
+        compiler_params=pltpu.CompilerParams(vmem_limit_bytes=16 * 1024 * 1024),
+    )(target, matrix)
+
+
 def condense_kernel(
-    incoming_ref, level_ref, slot_ref, target_ref, out_ref, matrix_ref, interior_ref, level_sem
+    arrived_ref, matrix_ref, slot_ref, target_ref, out_ref, incoming_ref, interior_ref, in_sem
 ):
     slots, cases, rows = incoming_ref.shape
     most = matrix_ref.shape[1] // rows
-    width = most * rows // CHUNKS
-    chunks = []
-    for c in range(CHUNKS):
-        part = (slice(None), slice(c * width, (c + 1) * width))
-        chunks.append(pltpu.make_async_copy(level_ref.at[part], matrix_ref.at[part], level_sem.at[c]))
-        chunks[c].start()
+    arriving = pltpu.make_async_copy(arrived_ref, incoming_ref, in_sem)
+    arriving.start()
     interior_ref[...] = jnp.zeros_like(interior_ref)
+    arriving.wait()
     marks = incoming_ref[:, 0:16, :].astype(F32)[:, 0, 0:1]
     filled = (marks < EMPTY / 2).astype(F32)
     row, col = iota((slots, LANES), 0), iota((slots, LANES), 1)
@@ -95,11 +105,7 @@
     for q in range(slots):
         at = pl.multiple_of(place[0, q], rows)
         interior_ref[0:cases, pl.ds(at, rows)] = incoming_ref[q]
-    boundary = jnp.zeros((matrix_ref.shape[0], LANES), F32)
-    for c in range(CHUNKS):
-        chunks[c].wait()
-        span = slice(c * width, (c + 1) * width)
-        boundary += dot_nt(matrix_ref[:, span], interior_ref[:, span])
+    boundary = dot_nt(matrix_ref[...], interior_ref[:, 0 : most * rows])
     parts = cases // 2
     lane = iota(boundary.shape, 1)
     dest = target_ref[...] // rows
@@ -123,12 +129,12 @@
     return pl.pallas_call(
         condense_kernel,
         out_shape=jax.ShapeDtypeStruct((members * RC, LANES), BF16),
-        in_specs=[VMEM, ANY, VMEM, VMEM],
+        in_specs=[ANY, VMEM, VMEM, VMEM],
         out_specs=VMEM,
         scratch_shapes=[
-            pltpu.VMEM(matrix.shape, BF16),
+            pltpu.VMEM(incoming.shape, BF16),
             pltpu.VMEM((LANES, depth + rows), BF16),
-            pltpu.SemaphoreType.DMA((CHUNKS,)),
+            pltpu.SemaphoreType.DMA,
         ],
         compiler_params=ROOMY,
     )(incoming, matrix, slot, target)
@@ -227,7 +233,7 @@
     outgoing = pack(block_owner, pressure, members)
     incoming = exchange(outgoing, "se")
 
-    target = level_one_map[0]
+    target = plan(level_one_map, level_one[0])[0]
     dest = target // half
     dofs = jnp.arange(target.shape[0], dtype=I32)
     earlier = (dest[:, None] == dest[None, :]) & (dofs[:, None] < dofs[None, :])

time: 98.2 us -> 97.6 us (level)
  no operation moved by 1% of the time
where the time goes in v4:
time: 97.6 us; the launch traced here: 97.2 us
  blocking collectives  31.8 us (33%)
  waiting for transfers between devices  30.3 us (31%)
  starting transfers between devices  25.8 us (26%)
  Pallas kernels  8.21 us (8%)
    all_to_all x2, blocking collectives, exchange(): return lax.all_to_all(x, axis, split_axis=0, concat_axis=0, tiled=True)  31.8 us
    all_to_all x2, starting transfers between devices, exchange(): return lax.all_to_all(x, axis, split_axis=0, concat_axis=0, tiled=True)  22.7 us
    ppermute x1, waiting for transfers between devices, local(): lax.ppermute(level_two[0], 'se', [(i, i ^ 1) for i in range(members)])  21 us
    all_to_all x2, waiting for transfers between devices, exchange(): return lax.all_to_all(x, axis, split_axis=0, concat_axis=0, tiled=True)  9.31 us
    pallas_call x1, Pallas kernels, condense(): pl.pallas_call(condense_kernel, out_shape=jax.ShapeDtypeStruct((members *...  3.9 us
    ppermute x1, starting transfers between devices, local(): lax.ppermute(level_two[0], 'se', [(i, i ^ 1) for i in range(members)])  3.06 us
    pallas_call x1, Pallas kernels, pack(): pl.pallas_call(pack_kernel, out_shape=jax.ShapeDtypeStruct((members * CAP...  2.3 us
  transfers between devices with their start and end apart: 3, of which 3 were waited for; matrix products, arithmetic and copies ran while one was open for 0% of the time, Pallas kernels for 0%

profile of v4, /device:TPU:1, one launch (start us, length us, event | category | flops | bytes accessed | tf_op | source)
XLA Modules:
  0.0 97.2 jit_solution(5305168185812606946)
XLA Ops:
  0.6 0.0 copy-start
  0.6 0.0 copy-start.2
  0.7 0.0 copy-start.1
  0.7 0.0 copy-start.3
  0.7 2.3 %shard_map.77 = bf16[64,64,128]{2,1,0:T(8,128)(2,1)} custom-call(s32[24]{0:T(128)} %owner_ref.1, bf16[24,64,128]{2,1,0:T(8,128)(2,1)} %pressure_ref.1), custom_call_target="tpu_custom_call" | custom-call | tf_op jit(solution)/shard_map/pallas_call | solution.py:60
  3.0 13.9 %all-to-all-start = ((bf16[64,64,128]{2,1,0:T(8,128)(2,1)}), bf16[64,64,128]{2,1,0:T(8,128)(2,1)}, u32[]{:S(2)}, u32[]{:S(2)}) async-start(bf16[64,64,128]{2,1,0:T(8,128)(2,1)} %shard_map.77), calls=%async_computation | async-start | bytes 2097152 | tf_op jit(solution)/shard_map/all_to_all | solution.py:223
  16.8 0.0 copy-done.2
  16.9 3.1 %collective-permute-start = (bf16[128,128]{1,0:T(8,128)(2,1)S(1)}, bf16[128,128]{1,0:T(8,128)(2,1)S(1)}, u32[]{:S(2)}, u32[]{:S(2)}) collective-permute-start(bf16[128,128]{1,0:T(8,128)(2,1)S(1)} %bitcast.18), channel_id=1, source_target_pairs={{0,1},{1,0},{2,3},{3,2},{4,5},{5,4},{6,7},{7,6},{8,9},{9,8},{10,11... | collective-permute-start | bytes 98312 | tf_op jit(solution)/shard_map/ppermute | solution.py:243
  19.9 0.0 copy-done.1
  19.9 0.0 copy-done.3
  20.0 0.1 convert_reduce_fusion
  20.1 21.0 %collective-permute-done.other_ref = bf16[128,128]{1,0:T(8,128)(2,1)S(1)} collective-permute-done((bf16[128,128]{1,0:T(8,128)(2,1)S(1)}, bf16[128,128]{1,0:T(8,128)(2,1)S(1)}, u32[]{:S(2)}, u32[]{:S(2)}) %collective-permute-start) | collective-permute-done | bytes 32800 | tf_op jit(solution)/shard_map/ppermute | solution.py:243
  41.1 0.1 copy.9.target_ref
  41.3 0.2 all-to-all-done.arrived_ref
  41.4 3.9 %shard_map.79 = bf16[512,128]{1,0:T(8,128)(2,1)} custom-call(bf16[64,64,128]{2,1,0:T(8,128)(2,1)} %all-to-all-done.arrived_ref, bf16[256,6144]{1,0:T(8,128)(2,1)S(1)} %bitcast.15, s32[1,256]{1,0:T(1,128)S(1)} %multiply_add_fusion.slot_ref, s32[256,1]{1,0:T(8,128)S(1)} %copy.9.target_ref), custom_call_target="tpu_custom_call" | custom-call | tf_op jit(solution)/shard_map/pallas_call | solution.py:129
  45.4 8.9 %all-to-all-start.1 = ((bf16[32,16,128]{2,1,0:T(8,128)(2,1)}), bf16[32,16,128]{2,1,0:T(8,128)(2,1)S(1)}, u32[]{:S(2)}, u32[]{:S(2)}) async-start(bf16[32,16,128]{2,1,0:T(8,128)(2,1)} %bitcast.7), calls=%async_computation.1 | async-start | bytes 262144 | tf_op jit(solution)/shard_map/all_to_all | solution.py:223
  54.3 0.0 copy-done
  54.3 9.1 %all-to-all-done.1 = bf16[32,16,128]{2,1,0:T(8,128)(2,1)S(1)} async-done(((bf16[32,16,128]{2,1,0:T(8,128)(2,1)}), bf16[32,16,128]{2,1,0:T(8,128)(2,1)S(1)}, u32[]{:S(2)}, u32[]{:S(2)}) %all-to-all-start.1) | async-done | bytes 131104 | tf_op jit(solution)/shard_map/all_to_all | solution.py:223
  63.4 0.9 shard_map.80
  64.3 19.3 %all_to_all.20.parts_ref = bf16[16,40,128]{2,1,0:T(8,128)(2,1)S(1)} all-to-all(bf16[16,40,128]{2,1,0:T(8,128)(2,1)S(1)} %get-tuple-element.9), channel_id=1, replica_groups=mesh['grp'=16,'se'=32] {'grp'}, dimensions={0} | all-to-all | bytes 327680 | tf_op jit(solution)/shard_map/all_to_all | solution.py:223
  83.6 0.5 shard_map.81
  84.1 12.5 %all_to_all.21.shares_ref = f32[32,8,128]{2,1,0:T(8,128)S(1)} all-to-all(f32[32,8,128]{2,1,0:T(8,128)S(1)} %bitcast.17), channel_id=1, replica_groups=mesh['grp'=16,'se'=32] {'se'}, dimensions={0} | all-to-all | bytes 262144 | tf_op jit(solution)/shard_map/all_to_all | solution.py:223
  96.6 0.6 shard_map.82
  (5 shorter events, 0.0 us)
Async XLA Ops:
  0.6 53.6 %copy-start = (s32[1,16,128]{2,1,0:T(8,128)S(1)}, s32[1,16,128]{2,1,0:T(8,128)}, u32[]{:S(2)}) copy-start(s32[1,16,128]{2,1,0:T(8,128)} %param.11) | copy-start | bytes 24580
  0.6 16.2 %copy-start.2 = (bf16[1,128,128]{2,1,0:T(8,128)(2,1)S(1)}, bf16[1,128,128]{2,1,0:T(8,128)(2,1)}, u32[]{:S(2)}) copy-start(bf16[1,128,128]{2,1,0:T(8,128)(2,1)} %param.10) | copy-start | bytes 98308
  0.7 19.3 %copy-start.1 = (bf16[1,256,6144]{2,1,0:T(8,128)(2,1)S(1)}, bf16[1,256,6144]{2,1,0:T(8,128)(2,1)}, u32[]{:S(2)}) copy-start(bf16[1,256,6144]{2,1,0:T(8,128)(2,1)} %param.8) | copy-start | bytes 9437188
  0.7 19.3 %copy-start.3 = (s32[1,256]{1,0:T(1,128)S(1)}, s32[1,256]{1,0:T(1,128)}, u32[]{:S(2)}) copy-start(s32[1,256]{1,0:T(1,128)} %target_ref.1) | copy-start | bytes 3076
  3.0 38.5 %all-to-all-start = ((bf16[64,64,128]{2,1,0:T(8,128)(2,1)}), bf16[64,64,128]{2,1,0:T(8,128)(2,1)}, u32[]{:S(2)}, u32[]{:S(2)}) async-start(bf16[64,64,128]{2,1,0:T(8,128)(2,1)} %shard_map.77), calls=%async_computation | async-start | bytes 2097152 | tf_op jit(solution)/shard_map/all_to_all | solution.py:223
  16.9 24.3 %collective-permute-start = (bf16[128,128]{1,0:T(8,128)(2,1)S(1)}, bf16[128,128]{1,0:T(8,128)(2,1)S(1)}, u32[]{:S(2)}, u32[]{:S(2)}) collective-permute-start(bf16[128,128]{1,0:T(8,128)(2,1)S(1)} %bitcast.18), channel_id=1, source_target_pairs={{0,1},{1,0},{2,3},{3,2},{4,5},{5,4},{6,7},{7,6},{8,9},{9,8},{10,11... | collective-permute-start | bytes 98312 | tf_op jit(solution)/shard_map/ppermute | solution.py:243
  45.4 18.1 %all-to-all-start.1 = ((bf16[32,16,128]{2,1,0:T(8,128)(2,1)}), bf16[32,16,128]{2,1,0:T(8,128)(2,1)S(1)}, u32[]{:S(2)}, u32[]{:S(2)}) async-start(bf16[32,16,128]{2,1,0:T(8,128)(2,1)} %bitcast.7), calls=%async_computation.1 | async-start | bytes 262144 | tf_op jit(solution)/shard_map/all_to_all | solution.py:223

commit v5 on v4

--- a/solution.py
+++ b/solution.py
@@ -140,11 +140,9 @@
     )(incoming, matrix, slot, target)
 
 
-def assemble_kernel(side_ref, rows_ref, matrix_ref, other_ref, root_ref, load_ref, out_ref):
+def assemble_kernel(side_ref, rows_ref, matrix_ref, other_ref, load_ref, out_ref):
     cases = load_ref.shape[0]
     parts = cases // 2
-    groups = out_ref.shape[0]
-    span = ROOT // groups
     rows = rows_ref[...]
     offsets = rows.astype(F32)[:, cases + parts : cases + parts + 2]
     want = (iota(rows.shape, 1) + 1).astype(F32)
@@ -153,66 +151,71 @@
     load_ref[...] = load
     second = dot_nt(load.astype(BF16), matrix_ref[...])
     second = jnp.where(side_ref[0] == 0, second[0:parts], second[parts:cases])
-    second = (second + dot_nt(other.astype(BF16), other_ref[...])).astype(BF16)
-    root = root_ref[...]
-    for g in range(groups):
-        out_ref[g, 0:parts, :] = second
-        within = root - g * span
-        index = jnp.where((within >= 0) & (within < span), within, 2 * span).astype(F32)
-        out_ref[g, parts : parts + 8, :] = jnp.broadcast_to(index, (8, LANES)).astype(BF16)
-
-
-def assemble(side, rows, matrix, other, root, cases, groups):
+    out_ref[...] = (second + dot_nt(other.astype(BF16), other_ref[...])).astype(BF16)
+
+
+def assemble(side, rows, matrix, other, cases):
     half = matrix.shape[1]
     return pl.pallas_call(
         assemble_kernel,
         out_shape=(
             jax.ShapeDtypeStruct((cases, half), F32),
-            jax.ShapeDtypeStruct((groups, cases // 2 + 8, LANES), BF16),
+            jax.ShapeDtypeStruct((cases // 2, LANES), BF16),
         ),
-        in_specs=[SMEM, VMEM, VMEM, VMEM, VMEM],
+        in_specs=[SMEM, VMEM, VMEM, VMEM],
         out_specs=(VMEM, VMEM),
         compiler_params=LIMIT,
-    )(side, rows, matrix, other, root)
-
-
-def root_kernel(side_ref, parts_ref, out_ref):
-    groups, depth, _ = parts_ref.shape
-    parts = depth - 8
-    span = out_ref.shape[0]
-    want = iota((span, LANES), 0).astype(F32)
-    total = jnp.zeros((span, parts), F32)
-    for g in range(groups):
-        index = parts_ref[g, parts:depth, :].astype(F32)[0:1]
-        total += dot_nt(one_hot(want == index), parts_ref[g, 0:parts, :])
-    zero = jnp.zeros_like(total)
-    first = side_ref[0] == 0
-    out_ref[:, 0:parts] = jnp.where(first, total, zero)
-    out_ref[:, parts : 2 * parts] = jnp.where(first, zero, total)
-    out_ref[:, 2 * parts :] = jnp.zeros((span, LANES - 2 * parts), F32)
-
-
-def root_sum(side, parts, span):
+    )(side, rows, matrix, other)
+
+
+def root_kernel(key_ref, mine_ref, theirs_ref, out_ref):
+    rows = out_ref.shape[0]
+    parts = mine_ref.shape[0]
+    share = LANES // parts
+    row = iota((rows, LANES), 0)
+    both = jnp.concatenate([mine_ref[...], theirs_ref[...]], axis=1)
+    zero = jnp.zeros_like(both)
+    total = jnp.zeros(out_ref.shape, F32)
+    for k in range(share):
+        hits = [one_hot(row * share + k == key_ref[c : c + 1, :]) for c in range(2)]
+        placed = jnp.concatenate([both if j == k else zero for j in range(share)], axis=0)
+        total += dot_nt(jnp.concatenate(hits, axis=1), placed)
+    out_ref[...] = total.astype(BF16)
+
+
+def root_sum(key, mine, theirs, rows):
     return pl.pallas_call(
         root_kernel,
-        out_shape=jax.ShapeDtypeStruct((span, LANES), F32),
-        in_specs=[SMEM, VMEM],
+        out_shape=jax.ShapeDtypeStruct((rows, LANES), BF16),
+        in_specs=[VMEM, VMEM, VMEM],
         out_specs=VMEM,
         compiler_params=LIMIT,
-    )(side, parts)
+    )(key, mine, theirs)
 
 
 def last_kernel(shares_ref, out_ref):
-    total = shares_ref[0]
-    for s in range(1, shares_ref.shape[0]):
-        total += shares_ref[s]
-    out_ref[...] = total[:, 0 : out_ref.shape[1]]
-
-
-def last_sum(shares, cases):
+    columns, cases = out_ref.shape
+    parts = cases // 2
+    share = LANES // parts
+    each = columns // share
+    period = 2 * each
+    total = jnp.zeros((16, LANES), F32)
+    for s in range(shares_ref.shape[0] // 16):
+        total += shares_ref[16 * s : 16 * s + 16, :].astype(F32)
+    halves = total[0:period]
+    for s in range(1, 16 // period):
+        halves += total[s * period : (s + 1) * period]
+    for k in range(share):
+        lanes = halves[:, k * parts : (k + 1) * parts]
+        both = jnp.concatenate([lanes[0:each], lanes[each:period]], axis=1)
+        for i in range(each):
+            out_ref[i * share + k : i * share + k + 1, :] = both[i : i + 1]
+
+
+def last_sum(shares, columns, cases):
     return pl.pallas_call(
         last_kernel,
-        out_shape=jax.ShapeDtypeStruct((shares.shape[1], cases), F32),
+        out_shape=jax.ShapeDtypeStruct((columns, cases), F32),
         in_specs=[VMEM],
         out_specs=VMEM,
         compiler_params=LIMIT,
@@ -225,7 +228,8 @@
 
 def local(pressure, block_owner, level_one, level_one_map, level_two, level_two_map):
     members = lax.axis_size("se")
-    groups = lax.axis_size("grp")
+    groups = lax.axis_size("y") * lax.axis_size("core")
+    core = lax.axis_index("core")
     member = lax.axis_index("se")
     cases = pressure.shape[1]
     half = level_two.shape[2]
@@ -241,32 +245,40 @@
     root = lax.dynamic_index_in_dim(level_two_map[0], member // 2, 0, keepdims=True)
     side = (member % 2)[None]
     partner = lax.ppermute(level_two[0], "se", [(i, i ^ 1) for i in range(members)])
-    target, partner = lax.optimization_barrier((target, partner))
+    span = ROOT // groups
+    roots = jnp.concatenate([root, lax.ppermute(root, "core", [(0, 1), (1, 0)])], axis=0)
+    group = roots // span
+    key = jnp.where(group % 2 == core, group // 2 * span + roots % span, -1)
+    target, partner, key = lax.optimization_barrier((target, partner, key))
 
     packed = condense(incoming, level_one[0], slot[None, :], target[:, None], members)
     received = exchange(packed.reshape(members, RC, LANES), "se").reshape(members * RC, LANES)
-    level_two_load, parts = assemble(side, received, level_two[0], partner, root, cases, groups)
-    parts = exchange(parts, "grp")
-    span = ROOT // groups
-    share = root_sum(side, parts, span)
-    share = exchange(share.reshape(members, span // members, LANES), "se")
-    root_load = last_sum(share, cases).T
+    level_two_load, second = assemble(side, received, level_two[0], partner, cases)
+    theirs = lax.ppermute(second, "core", [(0, 1), (1, 0)])
+    columns = span // members
+    share = root_sum(key, second, theirs, groups // 2 * span * (cases // 2) // LANES)
+    share = exchange(share, ("y", "se"))
+    root_load = last_sum(share, columns, cases).T
     return (level_two_load[None], root_load)
 
 
 def solution(mesh):
+    groups, members = mesh.devices.shape
+    split = jax.sharding.Mesh(mesh.devices.reshape(groups // 2, 2, members), ("y", "core", "se"))
+    grp = ("y", "core")
+    every = ("y", "core", "se")
     placed = (
-        P(("grp", "se"), None, None),
-        P(("grp", "se")),
-        P(("grp", "se"), None, None),
-        P(("grp", "se"), None),
-        P("grp", None, "se"),
-        P("grp", None, None),
+        P(every, None, None),
+        P(every),
+        P(every, None, None),
+        P(every, None),
+        P(grp, None, "se"),
+        P(grp, None, None),
     )
     return jax.shard_map(
         local,
-        mesh=mesh,
+        mesh=split,
         in_specs=placed,
-        out_specs=(P("grp", None, "se"), P(None, ("grp", "se"))),
+        out_specs=(P(grp, None, "se"), P(None, every)),
         check_vma=False,
     )

time: 97.6 us -> 96.2 us (0.986)
  starting transfers between devices: 25.8 us -> 33.9 us
  blocking collectives: 31.8 us -> 24.9 us
  waiting for transfers between devices: 30.3 us -> 27.6 us
    ppermute x0 -> x2, starting transfers between devices: none -> 8.1 us  [the longest x1 4.68 us: local(): theirs = lax.ppermute(second, 'core', [(0, 1), (1, 0)])]
    all_to_all x2 -> x1, blocking collectives: 31.8 us -> 24.9 us  [exchange(): return lax.all_to_all(x, axis, split_axis=0, concat_axis=0, tiled=True)]
    ppermute x1, waiting for transfers between devices: 21 us -> 16.9 us  [local(): lax.ppermute(level_two[0], 'se', [(i, i ^ 1) for i in range(members)])]
    ppermute x0 -> x2, waiting for transfers between devices: none -> 1.4 us  [the longest x1 0.81 us: local(): theirs = lax.ppermute(second, 'core', [(0, 1), (1, 0)])]
  transfers between devices with their start and end apart: 3 -> 5, of which waited for: 3 -> 5; matrix products, arithmetic and copies ran while one was open for 0% -> 0% of each run, Pallas kernels for 0% -> 0%
where the time goes in v5:
time: 96.2 us; the launch traced here: 95.8 us
  starting transfers between devices  33.9 us (35%)
  waiting for transfers between devices  27.6 us (29%)
  blocking collectives  24.9 us (26%)
  Pallas kernels  8.21 us (9%)
    all_to_all x1, blocking collectives, exchange(): return lax.all_to_all(x, axis, split_axis=0, concat_axis=0, tiled=True)  24.9 us
    all_to_all x2, starting transfers between devices, exchange(): return lax.all_to_all(x, axis, split_axis=0, concat_axis=0, tiled=True)  22.7 us
    ppermute x1, waiting for transfers between devices, local(): lax.ppermute(level_two[0], 'se', [(i, i ^ 1) for i in range(members)])  16.9 us
    all_to_all x2, waiting for transfers between devices, exchange(): return lax.all_to_all(x, axis, split_axis=0, concat_axis=0, tiled=True)  9.35 us
    ppermute x1, starting transfers between devices, local(): theirs = lax.ppermute(second, 'core', [(0, 1), (1, 0)])  4.68 us
    pallas_call x1, Pallas kernels, condense(): pl.pallas_call(condense_kernel, out_shape=jax.ShapeDtypeStruct((members *...  3.91 us
    ppermute x1, starting transfers between devices, local(): lax.ppermute(root, 'core', [(0, 1), (1, 0)])  3.42 us
    ppermute x1, starting transfers between devices, local(): lax.ppermute(level_two[0], 'se', [(i, i ^ 1) for i in range(members)])  3.06 us
  transfers between devices with their start and end apart: 5, of which 5 were waited for; matrix products, arithmetic and copies ran while one was open for 0% of the time, Pallas kernels for 0%

profile of v5, /device:TPU:1, one launch (start us, length us, event | category | flops | bytes accessed | tf_op | source)
XLA Modules:
  0.0 95.8 jit_solution(4426689342257441664)
XLA Ops:
  0.6 0.0 copy-start
  0.6 0.0 copy-start.2
  0.7 0.0 copy-start.1
  0.7 0.0 copy-start.3
  0.7 2.3 %shard_map.77 = bf16[64,64,128]{2,1,0:T(8,128)(2,1)} custom-call(s32[24]{0:T(128)} %owner_ref.1, bf16[24,64,128]{2,1,0:T(8,128)(2,1)} %pressure_ref.1), custom_call_target="tpu_custom_call" | custom-call | tf_op jit(solution)/shard_map/pallas_call | solution.py:60
  3.0 13.9 %all-to-all-start = ((bf16[64,64,128]{2,1,0:T(8,128)(2,1)}), bf16[64,64,128]{2,1,0:T(8,128)(2,1)}, u32[]{:S(2)}, u32[]{:S(2)}) async-start(bf16[64,64,128]{2,1,0:T(8,128)(2,1)} %shard_map.77), calls=%async_computation | async-start | bytes 2097152 | tf_op jit(solution)/shard_map/all_to_all | solution.py:226
  16.8 0.0 copy-done.2
  16.8 3.1 %collective-permute-start = (bf16[128,128]{1,0:T(8,128)(2,1)S(1)}, bf16[128,128]{1,0:T(8,128)(2,1)S(1)}, u32[]{:S(2)}, u32[]{:S(2)}) collective-permute-start(bf16[128,128]{1,0:T(8,128)(2,1)S(1)} %bitcast.20), channel_id=1, source_target_pairs={{0,1},{1,0},{2,3},{3,2},{4,5},{5,4},{6,7},{7,6},{8,9},{9,8},{10,11... | collective-permute-start | bytes 98312 | tf_op jit(solution)/shard_map/ppermute | solution.py:247
  19.9 0.0 copy-done
  20.0 3.4 %collective-permute-start.1 = (s32[1,128]{1,0:T(1,128)S(1)}, s32[1,128]{1,0:T(1,128)S(1)}, u32[]{:S(2)}, u32[]{:S(2)}) collective-permute-start(s32[1,128]{1,0:T(1,128)S(1)} %dynamic-slice_bitcast_fusion), channel_id=1, source_target_pairs={{0,32},{32,0},{1,33},{33,1},{2,34},{34,2},{3,35},{35,3},{4,36},{36... | collective-permute-start | bytes 1544 | tf_op jit(solution)/shard_map/ppermute | solution.py:249
  23.4 0.0 copy-done.1
  23.4 0.0 copy-done.3
  23.5 0.1 convert_reduce_fusion
  23.6 0.6 collective-permute-done.1
  24.2 16.9 %collective-permute-done.other_ref = bf16[128,128]{1,0:T(8,128)(2,1)S(1)} collective-permute-done((bf16[128,128]{1,0:T(8,128)(2,1)S(1)}, bf16[128,128]{1,0:T(8,128)(2,1)S(1)}, u32[]{:S(2)}, u32[]{:S(2)}) %collective-permute-start) | collective-permute-done | bytes 32800 | tf_op jit(solution)/shard_map/ppermute | solution.py:247
  41.1 0.1 copy.9.target_ref
  41.3 0.2 all-to-all-done.arrived_ref
  41.4 3.9 %shard_map.79 = bf16[512,128]{1,0:T(8,128)(2,1)} custom-call(bf16[64,64,128]{2,1,0:T(8,128)(2,1)} %all-to-all-done.arrived_ref, bf16[256,6144]{1,0:T(8,128)(2,1)S(1)} %bitcast.16, s32[1,256]{1,0:T(1,128)S(1)} %multiply_add_fusion.slot_ref, s32[256,1]{1,0:T(8,128)S(1)} %copy.9.target_ref), custom_call_target="tpu_custom_call" | custom-call | tf_op jit(solution)/shard_map/pallas_call | solution.py:129
  45.4 8.9 %all-to-all-start.1 = ((bf16[32,16,128]{2,1,0:T(8,128)(2,1)}), bf16[32,16,128]{2,1,0:T(8,128)(2,1)S(1)}, u32[]{:S(2)}, u32[]{:S(2)}) async-start(bf16[32,16,128]{2,1,0:T(8,128)(2,1)} %bitcast.8), calls=%async_computation.1 | async-start | bytes 262144 | tf_op jit(solution)/shard_map/all_to_all | solution.py:226
  54.2 9.2 %all-to-all-done.1 = bf16[32,16,128]{2,1,0:T(8,128)(2,1)S(1)} async-done(((bf16[32,16,128]{2,1,0:T(8,128)(2,1)}), bf16[32,16,128]{2,1,0:T(8,128)(2,1)S(1)}, u32[]{:S(2)}, u32[]{:S(2)}) %all-to-all-start.1) | async-done | bytes 131104 | tf_op jit(solution)/shard_map/all_to_all | solution.py:226
  63.4 0.9 shard_map.80
  64.3 4.7 %collective-permute-start.2 = (bf16[32,128]{1,0:T(8,128)(2,1)S(1)}, bf16[32,128]{1,0:T(8,128)(2,1)S(1)}, u32[]{:S(2)}, u32[]{:S(2)}) collective-permute-start(bf16[32,128]{1,0:T(8,128)(2,1)S(1)} %get-tuple-element.11.mine_ref), channel_id=1, source_target_pairs={{0,32},{32,0},{1,33},{33,1},{2,34},{34,2},{3,35},{35,3},{4,36},{36... | collective-permute-start | bytes 24584 | tf_op jit(solution)/shard_map/ppermute | solution.py:257
  69.0 0.8 collective-permute-done.2.theirs_ref
  69.8 0.4 shard_map.81
  70.2 24.9 %all_to_all.21 = bf16[256,2,128]{2,1,0:T(2,128)(2,1)S(1)} all-to-all(bf16[256,2,128]{2,1,0:T(2,128)(2,1)S(1)} %bitcast.18), channel_id=1, replica_groups=mesh['y'=8,'core'=2,'se'=32] {'y','se'}, dimensions={0} | all-to-all | bytes 262144 | tf_op jit(solution)/shard_map/all_to_all | solution.py:226
  95.1 0.7 shard_map.82
  (6 shorter events, 0.1 us)
Async XLA Ops:
  0.6 19.3 %copy-start = (s32[1,16,128]{2,1,0:T(8,128)S(1)}, s32[1,16,128]{2,1,0:T(8,128)}, u32[]{:S(2)}) copy-start(s32[1,16,128]{2,1,0:T(8,128)} %param.11) | copy-start | bytes 24580
  0.6 16.2 %copy-start.2 = (bf16[1,128,128]{2,1,0:T(8,128)(2,1)S(1)}, bf16[1,128,128]{2,1,0:T(8,128)(2,1)}, u32[]{:S(2)}) copy-start(bf16[1,128,128]{2,1,0:T(8,128)(2,1)} %param.10) | copy-start | bytes 98308
  0.7 22.7 %copy-start.1 = (bf16[1,256,6144]{2,1,0:T(8,128)(2,1)S(1)}, bf16[1,256,6144]{2,1,0:T(8,128)(2,1)}, u32[]{:S(2)}) copy-start(bf16[1,256,6144]{2,1,0:T(8,128)(2,1)} %param.8) | copy-start | bytes 9437188
  0.7 22.7 %copy-start.3 = (s32[1,256]{1,0:T(1,128)S(1)}, s32[1,256]{1,0:T(1,128)}, u32[]{:S(2)}) copy-start(s32[1,256]{1,0:T(1,128)} %target_ref.1) | copy-start | bytes 3076
  3.0 38.5 %all-to-all-start = ((bf16[64,64,128]{2,1,0:T(8,128)(2,1)}), bf16[64,64,128]{2,1,0:T(8,128)(2,1)}, u32[]{:S(2)}, u32[]{:S(2)}) async-start(bf16[64,64,128]{2,1,0:T(8,128)(2,1)} %shard_map.77), calls=%async_computation | async-start | bytes 2097152 | tf_op jit(solution)/shard_map/all_to_all | solution.py:226
  16.8 24.3 %collective-permute-start = (bf16[128,128]{1,0:T(8,128)(2,1)S(1)}, bf16[128,128]{1,0:T(8,128)(2,1)S(1)}, u32[]{:S(2)}, u32[]{:S(2)}) collective-permute-start(bf16[128,128]{1,0:T(8,128)(2,1)S(1)} %bitcast.20), channel_id=1, source_target_pairs={{0,1},{1,0},{2,3},{3,2},{4,5},{5,4},{6,7},{7,6},{8,9},{9,8},{10,11... | collective-permute-start | bytes 98312 | tf_op jit(solution)/shard_map/ppermute | solution.py:247
  20.0 4.2 %collective-permute-start.1 = (s32[1,128]{1,0:T(1,128)S(1)}, s32[1,128]{1,0:T(1,128)S(1)}, u32[]{:S(2)}, u32[]{:S(2)}) collective-permute-start(s32[1,128]{1,0:T(1,128)S(1)} %dynamic-slice_bitcast_fusion), channel_id=1, source_target_pairs={{0,32},{32,0},{1,33},{33,1},{2,34},{34,2},{3,35},{35,3},{4,36},{36... | collective-permute-start | bytes 1544 | tf_op jit(solution)/shard_map/ppermute | solution.py:249
  45.4 18.1 %all-to-all-start.1 = ((bf16[32,16,128]{2,1,0:T(8,128)(2,1)}), bf16[32,16,128]{2,1,0:T(8,128)(2,1)S(1)}, u32[]{:S(2)}, u32[]{:S(2)}) async-start(bf16[32,16,128]{2,1,0:T(8,128)(2,1)} %bitcast.8), calls=%async_computation.1 | async-start | bytes 262144 | tf_op jit(solution)/shard_map/all_to_all | solution.py:226
  64.3 5.5 %collective-permute-start.2 = (bf16[32,128]{1,0:T(8,128)(2,1)S(1)}, bf16[32,128]{1,0:T(8,128)(2,1)S(1)}, u32[]{:S(2)}, u32[]{:S(2)}) collective-permute-start(bf16[32,128]{1,0:T(8,128)(2,1)S(1)} %get-tuple-element.11.mine_ref), channel_id=1, source_target_pairs={{0,32},{32,0},{1,33},{33,1},{2,34},{34,2},{3,35},{35,3},{4,36},{36... | collective-permute-start | bytes 24584 | tf_op jit(solution)/shard_map/ppermute | solution.py:257

commit v6 on v5

--- a/solution.py
+++ b/solution.py
@@ -9,6 +9,7 @@
 CAPACITY = 2
 RC = 16
 LANES = 128
+EARLY = 3840
 EMPTY = 64.0
 BF16 = jnp.bfloat16
 F32 = jnp.float32
@@ -16,8 +17,8 @@
 VMEM = pl.BlockSpec(memory_space=pltpu.VMEM)
 SMEM = pl.BlockSpec(memory_space=pltpu.SMEM)
 ANY = pl.BlockSpec(memory_space=pl.ANY)
-WIDE = pltpu.CompilerParams(vmem_limit_bytes=60 * 1024 * 1024)
-ROOMY = pltpu.CompilerParams(vmem_limit_bytes=16 * 1024 * 1024)
+WIDE = pltpu.CompilerParams(vmem_limit_bytes=62 * 1024 * 1024)
+ROOMY = pltpu.CompilerParams(vmem_limit_bytes=50 * 1024 * 1024)
 LIMIT = pltpu.CompilerParams(vmem_limit_bytes=16 * 1024 * 1024)
 
 
@@ -73,29 +74,32 @@
     )(block_owner, pressure)
 
 
-def plan_kernel(target_ref, matrix_ref, out_ref):
-    out_ref[...] = target_ref[...]
-
-
-def plan(target, matrix):
-    return pl.pallas_call(
-        plan_kernel,
-        out_shape=jax.ShapeDtypeStruct(target.shape, I32),
-        in_specs=[VMEM, ANY],
-        out_specs=VMEM,
-        compiler_params=pltpu.CompilerParams(vmem_limit_bytes=16 * 1024 * 1024),
-    )(target, matrix)
+def bring_kernel(level_ref, out_ref, sem):
+    copy = pltpu.make_async_copy(level_ref.at[:, 0 : out_ref.shape[1]], out_ref, sem)
+    copy.start()
+    copy.wait()
+
+
+def bring(matrix):
+    return pl.pallas_call(
+        bring_kernel,
+        out_shape=jax.ShapeDtypeStruct((matrix.shape[0], EARLY), BF16),
+        in_specs=[ANY],
+        out_specs=VMEM,
+        scratch_shapes=[pltpu.SemaphoreType.DMA],
+        compiler_params=pltpu.CompilerParams(vmem_limit_bytes=48 * 1024 * 1024),
+    )(matrix)
 
 
 def condense_kernel(
-    arrived_ref, matrix_ref, slot_ref, target_ref, out_ref, incoming_ref, interior_ref, in_sem
+    incoming_ref, early_ref, level_ref, slot_ref, target_ref, out_ref, late_ref, interior_ref, level_sem
 ):
     slots, cases, rows = incoming_ref.shape
-    most = matrix_ref.shape[1] // rows
-    arriving = pltpu.make_async_copy(arrived_ref, incoming_ref, in_sem)
-    arriving.start()
+    depth = level_ref.shape[1]
+    most = depth // rows
+    late = pltpu.make_async_copy(level_ref.at[:, EARLY:depth], late_ref, level_sem)
+    late.start()
     interior_ref[...] = jnp.zeros_like(interior_ref)
-    arriving.wait()
     marks = incoming_ref[:, 0:16, :].astype(F32)[:, 0, 0:1]
     filled = (marks < EMPTY / 2).astype(F32)
     row, col = iota((slots, LANES), 0), iota((slots, LANES), 1)
@@ -105,7 +109,9 @@
     for q in range(slots):
         at = pl.multiple_of(place[0, q], rows)
         interior_ref[0:cases, pl.ds(at, rows)] = incoming_ref[q]
-    boundary = dot_nt(matrix_ref[...], interior_ref[:, 0 : most * rows])
+    boundary = dot_nt(early_ref[...], interior_ref[:, 0:EARLY])
+    late.wait()
+    boundary += dot_nt(late_ref[...], interior_ref[:, EARLY:depth])
     parts = cases // 2
     lane = iota(boundary.shape, 1)
     dest = target_ref[...] // rows
@@ -123,21 +129,21 @@
     out_ref[...] = sent.astype(BF16)
 
 
-def condense(incoming, matrix, slot, target, members):
+def condense(incoming, early, matrix, slot, target, members):
     depth = matrix.shape[1]
     rows = incoming.shape[2]
     return pl.pallas_call(
         condense_kernel,
         out_shape=jax.ShapeDtypeStruct((members * RC, LANES), BF16),
-        in_specs=[ANY, VMEM, VMEM, VMEM],
+        in_specs=[VMEM, VMEM, ANY, VMEM, VMEM],
         out_specs=VMEM,
         scratch_shapes=[
-            pltpu.VMEM(incoming.shape, BF16),
+            pltpu.VMEM((matrix.shape[0], depth - EARLY), BF16),
             pltpu.VMEM((LANES, depth + rows), BF16),
             pltpu.SemaphoreType.DMA,
         ],
         compiler_params=ROOMY,
-    )(incoming, matrix, slot, target)
+    )(incoming, early, matrix, slot, target)
 
 
 def assemble_kernel(side_ref, rows_ref, matrix_ref, other_ref, load_ref, out_ref):
@@ -237,7 +243,8 @@
     outgoing = pack(block_owner, pressure, members)
     incoming = exchange(outgoing, "se")
 
-    target = plan(level_one_map, level_one[0])[0]
+    target = level_one_map[0]
+    early = bring(level_one[0])
     dest = target // half
     dofs = jnp.arange(target.shape[0], dtype=I32)
     earlier = (dest[:, None] == dest[None, :]) & (dofs[:, None] < dofs[None, :])
@@ -249,9 +256,9 @@
     roots = jnp.concatenate([root, lax.ppermute(root, "core", [(0, 1), (1, 0)])], axis=0)
     group = roots // span
     key = jnp.where(group % 2 == core, group // 2 * span + roots % span, -1)
-    target, partner, key = lax.optimization_barrier((target, partner, key))
-
-    packed = condense(incoming, level_one[0], slot[None, :], target[:, None], members)
+    target, partner, key, early = lax.optimization_barrier((target, partner, key, early))
+
+    packed = condense(incoming, early, level_one[0], slot[None, :], target[:, None], members)
     received = exchange(packed.reshape(members, RC, LANES), "se").reshape(members * RC, LANES)
     level_two_load, second = assemble(side, received, level_two[0], partner, cases)
     theirs = lax.ppermute(second, "core", [(0, 1), (1, 0)])

time: 96.2 us -> 96.1 us (level)
  local copies, waits for them, and re-layouts: 0.16 us -> 2.04 us
  waiting for transfers between devices: 27.6 us -> 25.8 us
    unnamed x8, local copies, waits for them, and re-layouts: 0.02 us -> 1.9 us
    ppermute x1, waiting for transfers between devices: 16.9 us -> 15.7 us  [local(): lax.ppermute(level_two[0], 'se', [(i, i ^ 1) for i in range(members)])]
  transfers between devices with their start and end apart: 5 -> 5, of which waited for: 5 -> 4; matrix products, arithmetic and copies ran while one was open for 0% -> 0% of each run, Pallas kernels for 0% -> 0%
where the time goes in v6:
time: 96.1 us; the launch traced here: 95.6 us
  starting transfers between devices  33.6 us (35%)
  waiting for transfers between devices  25.8 us (27%)
  blocking collectives  24.9 us (26%)
  Pallas kernels  8.3 us (9%)
  local copies, waits for them, and re-layouts  2.04 us (2%)
    all_to_all x1, blocking collectives, exchange(): return lax.all_to_all(x, axis, split_axis=0, concat_axis=0, tiled=True)  24.9 us
    all_to_all x2, starting transfers between devices, exchange(): return lax.all_to_all(x, axis, split_axis=0, concat_axis=0, tiled=True)  22.6 us
    ppermute x1, waiting for transfers between devices, local(): lax.ppermute(level_two[0], 'se', [(i, i ^ 1) for i in range(members)])  15.7 us
    all_to_all x2, waiting for transfers between devices, exchange(): return lax.all_to_all(x, axis, split_axis=0, concat_axis=0, tiled=True)  9.35 us
    ppermute x1, starting transfers between devices, local(): theirs = lax.ppermute(second, 'core', [(0, 1), (1, 0)])  4.68 us
    pallas_call x1, Pallas kernels, condense(): pl.pallas_call(condense_kernel, out_shape=jax.ShapeDtypeStruct((members *...  4.02 us
    ppermute x1, starting transfers between devices, local(): lax.ppermute(level_two[0], 'se', [(i, i ^ 1) for i in range(members)])  3.42 us
    ppermute x1, starting transfers between devices, local(): lax.ppermute(root, 'core', [(0, 1), (1, 0)])  2.86 us
  transfers between devices with their start and end apart: 5, of which 4 were waited for; matrix products, arithmetic and copies ran while one was open for 0% of the time, Pallas kernels for 0%

profile of v6, /device:TPU:1, one launch (start us, length us, event | category | flops | bytes accessed | tf_op | source)
XLA Modules:
  0.0 95.6 jit_solution(16488445673461863850)
XLA Ops:
  0.6 0.0 copy-start
  0.6 0.0 copy-start.2
  0.7 0.0 copy-start.3
  0.7 2.1 %shard_map.77 = bf16[64,64,128]{2,1,0:T(8,128)(2,1)} custom-call(s32[24]{0:T(128)} %owner_ref.1, bf16[24,64,128]{2,1,0:T(8,128)(2,1)} %pressure_ref.1), custom_call_target="tpu_custom_call" | custom-call | tf_op jit(solution)/shard_map/pallas_call | solution.py:61
  2.8 13.7 %all-to-all-start = ((bf16[64,64,128]{2,1,0:T(8,128)(2,1)}), bf16[64,64,128]{2,1,0:T(8,128)(2,1)S(1)}, u32[]{:S(2)}, u32[]{:S(2)}) async-start(bf16[64,64,128]{2,1,0:T(8,128)(2,1)} %shard_map.77), calls=%async_computation | async-start | bytes 2097152 | tf_op jit(solution)/shard_map/all_to_all | solution.py:232
  16.5 0.0 copy-done
  16.6 2.9 %collective-permute-start.1 = (s32[1,128]{1,0:T(1,128)S(1)}, s32[1,128]{1,0:T(1,128)S(1)}, u32[]{:S(2)}, u32[]{:S(2)}) collective-permute-start(s32[1,128]{1,0:T(1,128)S(1)} %dynamic-slice_bitcast_fusion), channel_id=1, source_target_pairs={{0,32},{32,0},{1,33},{33,1},{2,34},{34,2},{3,35},{35,3},{4,36},{36... | collective-permute-start | bytes 1544 | tf_op jit(solution)/shard_map/ppermute | solution.py:256
  19.4 0.0 copy-done.2
  19.4 3.4 %collective-permute-start = (bf16[128,128]{1,0:T(8,128)(2,1)S(1)}, bf16[128,128]{1,0:T(8,128)(2,1)S(1)}, u32[]{:S(2)}, u32[]{:S(2)}) collective-permute-start(bf16[128,128]{1,0:T(8,128)(2,1)S(1)} %bitcast.20), channel_id=1, source_target_pairs={{0,1},{1,0},{2,3},{3,2},{4,5},{5,4},{6,7},{7,6},{8,9},{9,8},{10,11... | collective-permute-start | bytes 98312 | tf_op jit(solution)/shard_map/ppermute | solution.py:254
  22.9 0.0 copy-done.3
  22.9 0.1 convert_reduce_fusion
  23.0 0.0 copy-start.1
  23.0 1.9 %copy-done.1 = bf16[1,256,6144]{2,1,0:T(8,128)(2,1)S(1)} copy-done((bf16[1,256,6144]{2,1,0:T(8,128)(2,1)S(1)}, bf16[1,256,6144]{2,1,0:T(8,128)(2,1)}, u32[]{:S(2)}) %copy-start.1) | copy-done | bytes 3145752
  24.9 0.2 shard_map.78.early_ref
  25.1 0.0 collective-permute-done.1
  25.1 15.7 %collective-permute-done.other_ref = bf16[128,128]{1,0:T(8,128)(2,1)S(1)} collective-permute-done((bf16[128,128]{1,0:T(8,128)(2,1)S(1)}, bf16[128,128]{1,0:T(8,128)(2,1)S(1)}, u32[]{:S(2)}, u32[]{:S(2)}) %collective-permute-start) | collective-permute-done | bytes 32800 | tf_op jit(solution)/shard_map/ppermute | solution.py:254
  40.8 0.1 copy.9.target_ref
  40.9 0.2 all-to-all-done.incoming_ref
  41.1 4.0 %shard_map.79 = bf16[512,128]{1,0:T(8,128)(2,1)} custom-call(bf16[64,64,128]{2,1,0:T(8,128)(2,1)S(1)} %all-to-all-done.incoming_ref, bf16[256,3840]{1,0:T(8,128)(2,1)S(1)} %shard_map.78.early_ref, bf16[256,6144]{1,0:T(8,128)(2,1)} %bitcast.15, s32[1,256]{1,0:T(1,128)S(1)} %multiply_add_fusion.slot_ref, s32[256,1]{1,0:T(8,128)S(1)} %copy.9.target_ref), custom_call_target="tpu_custom_call" | custom-call | tf_op jit(solution)/shard_map/pallas_call | solution.py:135
  45.2 8.9 %all-to-all-start.1 = ((bf16[32,16,128]{2,1,0:T(8,128)(2,1)}), bf16[32,16,128]{2,1,0:T(8,128)(2,1)S(1)}, u32[]{:S(2)}, u32[]{:S(2)}) async-start(bf16[32,16,128]{2,1,0:T(8,128)(2,1)} %bitcast.8), calls=%async_computation.1 | async-start | bytes 262144 | tf_op jit(solution)/shard_map/all_to_all | solution.py:232
  54.1 9.2 %all-to-all-done.1 = bf16[32,16,128]{2,1,0:T(8,128)(2,1)S(1)} async-done(((bf16[32,16,128]{2,1,0:T(8,128)(2,1)}), bf16[32,16,128]{2,1,0:T(8,128)(2,1)S(1)}, u32[]{:S(2)}, u32[]{:S(2)}) %all-to-all-start.1) | async-done | bytes 131104 | tf_op jit(solution)/shard_map/all_to_all | solution.py:232
  63.2 0.9 shard_map.80
  64.1 4.7 %collective-permute-start.2 = (bf16[32,128]{1,0:T(8,128)(2,1)S(1)}, bf16[32,128]{1,0:T(8,128)(2,1)S(1)}, u32[]{:S(2)}, u32[]{:S(2)}) collective-permute-start(bf16[32,128]{1,0:T(8,128)(2,1)S(1)} %get-tuple-element.13.mine_ref), channel_id=1, source_target_pairs={{0,32},{32,0},{1,33},{33,1},{2,34},{34,2},{3,35},{35,3},{4,36},{36... | collective-permute-start | bytes 24584 | tf_op jit(solution)/shard_map/ppermute | solution.py:264
  68.8 0.8 collective-permute-done.2.theirs_ref
  69.6 0.4 shard_map.81
  70.0 24.9 %all_to_all.21 = bf16[256,2,128]{2,1,0:T(2,128)(2,1)S(1)} all-to-all(bf16[256,2,128]{2,1,0:T(2,128)(2,1)S(1)} %bitcast.18), channel_id=1, replica_groups=mesh['y'=8,'core'=2,'se'=32] {'y','se'}, dimensions={0} | all-to-all | bytes 262144 | tf_op jit(solution)/shard_map/all_to_all | solution.py:232
  94.9 0.7 shard_map.82
  (5 shorter events, 0.1 us)
Async XLA Ops:
  0.6 15.9 %copy-start = (s32[1,16,128]{2,1,0:T(8,128)S(1)}, s32[1,16,128]{2,1,0:T(8,128)}, u32[]{:S(2)}) copy-start(s32[1,16,128]{2,1,0:T(8,128)} %param.11) | copy-start | bytes 24580
  0.6 18.8 %copy-start.2 = (bf16[1,128,128]{2,1,0:T(8,128)(2,1)S(1)}, bf16[1,128,128]{2,1,0:T(8,128)(2,1)}, u32[]{:S(2)}) copy-start(bf16[1,128,128]{2,1,0:T(8,128)(2,1)} %param.10) | copy-start | bytes 98308
  0.7 22.2 %copy-start.3 = (s32[1,256]{1,0:T(1,128)S(1)}, s32[1,256]{1,0:T(1,128)}, u32[]{:S(2)}) copy-start(s32[1,256]{1,0:T(1,128)} %param.9) | copy-start | bytes 3076
  2.8 38.4 %all-to-all-start = ((bf16[64,64,128]{2,1,0:T(8,128)(2,1)}), bf16[64,64,128]{2,1,0:T(8,128)(2,1)S(1)}, u32[]{:S(2)}, u32[]{:S(2)}) async-start(bf16[64,64,128]{2,1,0:T(8,128)(2,1)} %shard_map.77), calls=%async_computation | async-start | bytes 2097152 | tf_op jit(solution)/shard_map/all_to_all | solution.py:232
  16.6 8.6 %collective-permute-start.1 = (s32[1,128]{1,0:T(1,128)S(1)}, s32[1,128]{1,0:T(1,128)S(1)}, u32[]{:S(2)}, u32[]{:S(2)}) collective-permute-start(s32[1,128]{1,0:T(1,128)S(1)} %dynamic-slice_bitcast_fusion), channel_id=1, source_target_pairs={{0,32},{32,0},{1,33},{33,1},{2,34},{34,2},{3,35},{35,3},{4,36},{36... | collective-permute-start | bytes 1544 | tf_op jit(solution)/shard_map/ppermute | solution.py:256
  19.4 21.4 %collective-permute-start = (bf16[128,128]{1,0:T(8,128)(2,1)S(1)}, bf16[128,128]{1,0:T(8,128)(2,1)S(1)}, u32[]{:S(2)}, u32[]{:S(2)}) collective-permute-start(bf16[128,128]{1,0:T(8,128)(2,1)S(1)} %bitcast.20), channel_id=1, source_target_pairs={{0,1},{1,0},{2,3},{3,2},{4,5},{5,4},{6,7},{7,6},{8,9},{9,8},{10,11... | collective-permute-start | bytes 98312 | tf_op jit(solution)/shard_map/ppermute | solution.py:254
  23.0 1.9 %copy-start.1 = (bf16[1,256,6144]{2,1,0:T(8,128)(2,1)S(1)}, bf16[1,256,6144]{2,1,0:T(8,128)(2,1)}, u32[]{:S(2)}) copy-start(bf16[1,256,6144]{2,1,0:T(8,128)(2,1)} %param.8) | copy-start | bytes 9437188
  45.2 18.1 %all-to-all-start.1 = ((bf16[32,16,128]{2,1,0:T(8,128)(2,1)}), bf16[32,16,128]{2,1,0:T(8,128)(2,1)S(1)}, u32[]{:S(2)}, u32[]{:S(2)}) async-start(bf16[32,16,128]{2,1,0:T(8,128)(2,1)} %bitcast.8), calls=%async_computation.1 | async-start | bytes 262144 | tf_op jit(solution)/shard_map/all_to_all | solution.py:232
  64.1 5.5 %collective-permute-start.2 = (bf16[32,128]{1,0:T(8,128)(2,1)S(1)}, bf16[32,128]{1,0:T(8,128)(2,1)S(1)}, u32[]{:S(2)}, u32[]{:S(2)}) collective-permute-start(bf16[32,128]{1,0:T(8,128)(2,1)S(1)} %get-tuple-element.13.mine_ref), channel_id=1, source_target_pairs={{0,32},{32,0},{1,33},{33,1},{2,34},{34,2},{3,35},{35,3},{4,36},{36... | collective-permute-start | bytes 24584 | tf_op jit(solution)/shard_map/ppermute | solution.py:264

commit v7 on v6

--- a/solution.py
+++ b/solution.py
@@ -256,7 +256,7 @@
     roots = jnp.concatenate([root, lax.ppermute(root, "core", [(0, 1), (1, 0)])], axis=0)
     group = roots // span
     key = jnp.where(group % 2 == core, group // 2 * span + roots % span, -1)
-    target, partner, key, early = lax.optimization_barrier((target, partner, key, early))
+    target, partner, key, side, early = lax.optimization_barrier((target, partner, key, side, early))
 
     packed = condense(incoming, early, level_one[0], slot[None, :], target[:, None], members)
     received = exchange(packed.reshape(members, RC, LANES), "se").reshape(members * RC, LANES)

time: 96.1 us -> 95.1 us (0.990)
  blocking collectives: 24.9 us -> 42.7 us
  waiting for transfers between devices: 25.8 us -> 16.6 us
  starting transfers between devices: 33.6 us -> 24.7 us
    all_to_all x1 -> x2, blocking collectives: 24.9 us -> 42.7 us  [exchange(): return lax.all_to_all(x, axis, split_axis=0, concat_axis=0, tiled=True)]
    all_to_all x2 -> x1, waiting for transfers between devices: 9.35 us -> 0.18 us  [exchange(): return lax.all_to_all(x, axis, split_axis=0, concat_axis=0, tiled=True)]
    all_to_all x2 -> x1, starting transfers between devices: 22.6 us -> 13.7 us  [exchange(): return lax.all_to_all(x, axis, split_axis=0, concat_axis=0, tiled=True)]
  transfers between devices with their start and end apart: 5 -> 4, of which waited for: 4 -> 3; matrix products, arithmetic and copies ran while one was open for 0% -> 0% of each run, Pallas kernels for 0% -> 0%
where the time goes in v7:
time: 95.1 us; the launch traced here: 94.7 us
  blocking collectives  42.7 us (45%)
  starting transfers between devices  24.7 us (26%)
  waiting for transfers between devices  16.6 us (17%)
  Pallas kernels  7.57 us (8%)
  local copies, waits for them, and re-layouts  2.04 us (2%)
    all_to_all x2, blocking collectives, exchange(): return lax.all_to_all(x, axis, split_axis=0, concat_axis=0, tiled=True)  42.7 us
    ppermute x1, waiting for transfers between devices, local(): lax.ppermute(level_two[0], 'se', [(i, i ^ 1) for i in range(members)])  15.6 us
    all_to_all x1, starting transfers between devices, exchange(): return lax.all_to_all(x, axis, split_axis=0, concat_axis=0, tiled=True)  13.7 us
    ppermute x1, starting transfers between devices, local(): theirs = lax.ppermute(second, 'core', [(0, 1), (1, 0)])  4.68 us
    ppermute x1, starting transfers between devices, local(): lax.ppermute(level_two[0], 'se', [(i, i ^ 1) for i in range(members)])  3.42 us
    pallas_call x1, Pallas kernels, condense(): pl.pallas_call(condense_kernel, out_shape=jax.ShapeDtypeStruct((members *...  3.29 us
    ppermute x1, starting transfers between devices, local(): lax.ppermute(root, 'core', [(0, 1), (1, 0)])  2.86 us
    pallas_call x1, Pallas kernels, pack(): pl.pallas_call(pack_kernel, out_shape=jax.ShapeDtypeStruct((members * CAP...  2.1 us
  transfers between devices with their start and end apart: 4, of which 3 were waited for; matrix products, arithmetic and copies ran while one was open for 0% of the time, Pallas kernels for 0%

profile of v7, /device:TPU:1, one launch (start us, length us, event | category | flops | bytes accessed | tf_op | source)
XLA Modules:
  0.0 94.7 jit_solution(11024229171682972539)
XLA Ops:
  0.6 0.0 copy-start
  0.6 0.0 copy-start.2
  0.7 0.0 copy-start.3
  0.7 2.1 %shard_map.78 = bf16[64,64,128]{2,1,0:T(8,128)(2,1)} custom-call(s32[24]{0:T(128)} %owner_ref.1, bf16[24,64,128]{2,1,0:T(8,128)(2,1)} %pressure_ref.1), custom_call_target="tpu_custom_call" | custom-call | tf_op jit(solution)/shard_map/pallas_call | solution.py:61
  2.8 13.7 %all-to-all-start = ((bf16[64,64,128]{2,1,0:T(8,128)(2,1)}), bf16[64,64,128]{2,1,0:T(8,128)(2,1)S(1)}, u32[]{:S(2)}, u32[]{:S(2)}) async-start(bf16[64,64,128]{2,1,0:T(8,128)(2,1)} %shard_map.78), calls=%async_computation | async-start | bytes 2097152 | tf_op jit(solution)/shard_map/all_to_all | solution.py:232
  16.5 0.0 copy-done
  16.6 2.9 %collective-permute-start.1 = (s32[1,128]{1,0:T(1,128)S(1)}, s32[1,128]{1,0:T(1,128)S(1)}, u32[]{:S(2)}, u32[]{:S(2)}) collective-permute-start(s32[1,128]{1,0:T(1,128)S(1)} %dynamic-slice_bitcast_fusion), channel_id=1, source_target_pairs={{0,32},{32,0},{1,33},{33,1},{2,34},{34,2},{3,35},{35,3},{4,36},{36... | collective-permute-start | bytes 1544 | tf_op jit(solution)/shard_map/ppermute | solution.py:256
  19.4 0.0 copy-done.2
  19.4 3.4 %collective-permute-start = (bf16[128,128]{1,0:T(8,128)(2,1)S(1)}, bf16[128,128]{1,0:T(8,128)(2,1)S(1)}, u32[]{:S(2)}, u32[]{:S(2)}) collective-permute-start(bf16[128,128]{1,0:T(8,128)(2,1)S(1)} %bitcast.21), channel_id=1, source_target_pairs={{0,1},{1,0},{2,3},{3,2},{4,5},{5,4},{6,7},{7,6},{8,9},{9,8},{10,11... | collective-permute-start | bytes 98312 | tf_op jit(solution)/shard_map/ppermute | solution.py:254
  22.9 0.0 copy-done.3
  22.9 0.1 convert_reduce_fusion
  23.1 0.0 copy-start.1
  23.1 1.9 %copy-done.1 = bf16[1,256,6144]{2,1,0:T(8,128)(2,1)S(1)} copy-done((bf16[1,256,6144]{2,1,0:T(8,128)(2,1)S(1)}, bf16[1,256,6144]{2,1,0:T(8,128)(2,1)}, u32[]{:S(2)}) %copy-start.1) | copy-done | bytes 3145752
  24.9 0.2 shard_map.77.early_ref
  25.1 0.0 collective-permute-done.1
  25.2 15.6 %collective-permute-done.other_ref = bf16[128,128]{1,0:T(8,128)(2,1)S(1)} collective-permute-done((bf16[128,128]{1,0:T(8,128)(2,1)S(1)}, bf16[128,128]{1,0:T(8,128)(2,1)S(1)}, u32[]{:S(2)}, u32[]{:S(2)}) %collective-permute-start) | collective-permute-done | bytes 32800 | tf_op jit(solution)/shard_map/ppermute | solution.py:254
  40.8 0.1 copy.9.target_ref
  41.0 0.2 all-to-all-done.incoming_ref
  41.1 3.3 %shard_map.79 = bf16[512,128]{1,0:T(8,128)(2,1)S(1)} custom-call(bf16[64,64,128]{2,1,0:T(8,128)(2,1)S(1)} %all-to-all-done.incoming_ref, bf16[256,3840]{1,0:T(8,128)(2,1)S(1)} %shard_map.77.early_ref, bf16[256,6144]{1,0:T(8,128)(2,1)} %bitcast.15, s32[1,256]{1,0:T(1,128)S(1)} %multiply_add_fusion.slot_ref, s32[256,1]{1,0:T(8,128)S(1)} %copy.9.target_ref), custom_call_target="tpu_custom_call" | custom-call | tf_op jit(solution)/shard_map/pallas_call | solution.py:135
  44.4 17.9 %all_to_all.21 = bf16[32,16,128]{2,1,0:T(8,128)(2,1)S(1)} all-to-all(bf16[32,16,128]{2,1,0:T(8,128)(2,1)S(1)} %bitcast.17), channel_id=1, replica_groups=mesh['y'=8,'core'=2,'se'=32] {'se'}, dimensions={0} | all-to-all | bytes 262144 | tf_op jit(solution)/shard_map/all_to_all | solution.py:232
  62.3 0.9 shard_map.80
  63.2 4.7 %collective-permute-start.2 = (bf16[32,128]{1,0:T(8,128)(2,1)S(1)}, bf16[32,128]{1,0:T(8,128)(2,1)S(1)}, u32[]{:S(2)}, u32[]{:S(2)}) collective-permute-start(bf16[32,128]{1,0:T(8,128)(2,1)S(1)} %get-tuple-element.15.mine_ref), channel_id=1, source_target_pairs={{0,32},{32,0},{1,33},{33,1},{2,34},{34,2},{3,35},{35,3},{4,36},{36... | collective-permute-start | bytes 24584 | tf_op jit(solution)/shard_map/ppermute | solution.py:264
  67.9 0.8 collective-permute-done.2.theirs_ref
  68.7 0.4 shard_map.81
  69.1 24.9 %all_to_all.22 = bf16[256,2,128]{2,1,0:T(2,128)(2,1)S(1)} all-to-all(bf16[256,2,128]{2,1,0:T(2,128)(2,1)S(1)} %bitcast.19), channel_id=1, replica_groups=mesh['y'=8,'core'=2,'se'=32] {'y','se'}, dimensions={0} | all-to-all | bytes 262144 | tf_op jit(solution)/shard_map/all_to_all | solution.py:232
  94.0 0.7 shard_map.82
  (5 shorter events, 0.1 us)
Async XLA Ops:
  0.6 15.9 %copy-start = (s32[1,16,128]{2,1,0:T(8,128)S(1)}, s32[1,16,128]{2,1,0:T(8,128)}, u32[]{:S(2)}) copy-start(s32[1,16,128]{2,1,0:T(8,128)} %param.11) | copy-start | bytes 24580
  0.6 18.8 %copy-start.2 = (bf16[1,128,128]{2,1,0:T(8,128)(2,1)S(1)}, bf16[1,128,128]{2,1,0:T(8,128)(2,1)}, u32[]{:S(2)}) copy-start(bf16[1,128,128]{2,1,0:T(8,128)(2,1)} %param.10) | copy-start | bytes 98308
  0.7 22.2 %copy-start.3 = (s32[1,256]{1,0:T(1,128)S(1)}, s32[1,256]{1,0:T(1,128)}, u32[]{:S(2)}) copy-start(s32[1,256]{1,0:T(1,128)} %param.9) | copy-start | bytes 3076
  2.8 38.4 %all-to-all-start = ((bf16[64,64,128]{2,1,0:T(8,128)(2,1)}), bf16[64,64,128]{2,1,0:T(8,128)(2,1)S(1)}, u32[]{:S(2)}, u32[]{:S(2)}) async-start(bf16[64,64,128]{2,1,0:T(8,128)(2,1)} %shard_map.78), calls=%async_computation | async-start | bytes 2097152 | tf_op jit(solution)/shard_map/all_to_all | solution.py:232
  16.6 8.6 %collective-permute-start.1 = (s32[1,128]{1,0:T(1,128)S(1)}, s32[1,128]{1,0:T(1,128)S(1)}, u32[]{:S(2)}, u32[]{:S(2)}) collective-permute-start(s32[1,128]{1,0:T(1,128)S(1)} %dynamic-slice_bitcast_fusion), channel_id=1, source_target_pairs={{0,32},{32,0},{1,33},{33,1},{2,34},{34,2},{3,35},{35,3},{4,36},{36... | collective-permute-start | bytes 1544 | tf_op jit(solution)/shard_map/ppermute | solution.py:256
  19.4 21.4 %collective-permute-start = (bf16[128,128]{1,0:T(8,128)(2,1)S(1)}, bf16[128,128]{1,0:T(8,128)(2,1)S(1)}, u32[]{:S(2)}, u32[]{:S(2)}) collective-permute-start(bf16[128,128]{1,0:T(8,128)(2,1)S(1)} %bitcast.21), channel_id=1, source_target_pairs={{0,1},{1,0},{2,3},{3,2},{4,5},{5,4},{6,7},{7,6},{8,9},{9,8},{10,11... | collective-permute-start | bytes 98312 | tf_op jit(solution)/shard_map/ppermute | solution.py:254
  23.1 1.9 %copy-start.1 = (bf16[1,256,6144]{2,1,0:T(8,128)(2,1)S(1)}, bf16[1,256,6144]{2,1,0:T(8,128)(2,1)}, u32[]{:S(2)}) copy-start(bf16[1,256,6144]{2,1,0:T(8,128)(2,1)} %param.8) | copy-start | bytes 9437188
  63.2 5.5 %collective-permute-start.2 = (bf16[32,128]{1,0:T(8,128)(2,1)S(1)}, bf16[32,128]{1,0:T(8,128)(2,1)S(1)}, u32[]{:S(2)}, u32[]{:S(2)}) collective-permute-start(bf16[32,128]{1,0:T(8,128)(2,1)S(1)} %get-tuple-element.15.mine_ref), channel_id=1, source_target_pairs={{0,32},{32,0},{1,33},{33,1},{2,34},{34,2},{3,35},{35,3},{4,36},{36... | collective-permute-start | bytes 24584 | tf_op jit(solution)/shard_map/ppermute | solution.py:264

commit v8 on v7

--- a/solution.py
+++ b/solution.py
@@ -9,7 +9,7 @@
 CAPACITY = 2
 RC = 16
 LANES = 128
-EARLY = 3840
+EARLY = 3072
 EMPTY = 64.0
 BF16 = jnp.bfloat16
 F32 = jnp.float32
@@ -123,9 +123,12 @@
     other = jnp.where((lane >= cases) & (lane < cases + parts), other, 0.0)
     other = jnp.where(lane == cases + parts + 1, offset, other)
     slot = slot_ref[...]
-    want = iota((out_ref.shape[0], slot.shape[1]), 0)
-    sent = jnp.dot(one_hot(slot == want), own.astype(BF16), preferred_element_type=F32)
-    sent += jnp.dot(one_hot(slot == want ^ RC), other.astype(BF16), preferred_element_type=F32)
+    choose = one_hot(slot == iota((out_ref.shape[0], slot.shape[1]), 0))
+    both = jnp.concatenate([own, other], axis=1).astype(BF16)
+    chosen = jnp.dot(choose, both, preferred_element_type=F32)
+    blocks = chosen[:, LANES : 2 * LANES].reshape(-1, 2, RC, LANES)
+    swapped = jnp.concatenate([blocks[:, 1:2], blocks[:, 0:1]], axis=1)
+    sent = chosen[:, 0:LANES] + swapped.reshape(-1, LANES)
     out_ref[...] = sent.astype(BF16)
 
 
@@ -152,8 +155,10 @@
     rows = rows_ref[...]
     offsets = rows.astype(F32)[:, cases + parts : cases + parts + 2]
     want = (iota(rows.shape, 1) + 1).astype(F32)
-    load = dot_tn(rows, one_hot(offsets[:, 0:1] == want))[0:cases]
-    other = dot_tn(rows, one_hot(offsets[:, 1:2] == want))[cases : cases + parts]
+    hits = jnp.concatenate([one_hot(offsets[:, 0:1] == want), one_hot(offsets[:, 1:2] == want)], axis=1)
+    loads = dot_tn(rows, hits)
+    load = loads[0:cases, 0:LANES]
+    other = loads[cases : cases + parts, LANES : 2 * LANES]
     load_ref[...] = load
     second = dot_nt(load.astype(BF16), matrix_ref[...])
     second = jnp.where(side_ref[0] == 0, second[0:parts], second[parts:cases])

time: 95.1 us -> 95.1 us (level)
  no operation moved by 1% of the time
where the time goes in v8:
time: 95.1 us; the launch traced here: 94.6 us
  blocking collectives  42.7 us (45%)
  starting transfers between devices  24.7 us (26%)
  waiting for transfers between devices  16.7 us (18%)
  Pallas kernels  7.53 us (8%)
  local copies, waits for them, and re-layouts  2.04 us (2%)
    all_to_all x2, blocking collectives, exchange(): return lax.all_to_all(x, axis, split_axis=0, concat_axis=0, tiled=True)  42.7 us
    ppermute x1, waiting for transfers between devices, local(): lax.ppermute(level_two[0], 'se', [(i, i ^ 1) for i in range(members)])  15.7 us
    all_to_all x1, starting transfers between devices, exchange(): return lax.all_to_all(x, axis, split_axis=0, concat_axis=0, tiled=True)  13.7 us
    ppermute x1, starting transfers between devices, local(): theirs = lax.ppermute(second, 'core', [(0, 1), (1, 0)])  4.69 us
    ppermute x1, starting transfers between devices, local(): lax.ppermute(level_two[0], 'se', [(i, i ^ 1) for i in range(members)])  3.42 us
    pallas_call x1, Pallas kernels, condense(): pl.pallas_call(condense_kernel, out_shape=jax.ShapeDtypeStruct((members *...  3.24 us
    ppermute x1, starting transfers between devices, local(): lax.ppermute(root, 'core', [(0, 1), (1, 0)])  2.86 us
    pallas_call x1, Pallas kernels, pack(): pl.pallas_call(pack_kernel, out_shape=jax.ShapeDtypeStruct((members * CAP...  2.1 us
  transfers between devices with their start and end apart: 4, of which 3 were waited for; matrix products, arithmetic and copies ran while one was open for 0% of the time, Pallas kernels for 0%

profile of v8, /device:TPU:1, one launch (start us, length us, event | category | flops | bytes accessed | tf_op | source)
XLA Modules:
  0.0 94.6 jit_solution(3054210469055333219)
XLA Ops:
  0.6 0.0 copy-start
  0.6 0.0 copy-start.2
  0.7 0.0 copy-start.3
  0.7 2.1 %shard_map.78 = bf16[64,64,128]{2,1,0:T(8,128)(2,1)} custom-call(s32[24]{0:T(128)} %owner_ref.1, bf16[24,64,128]{2,1,0:T(8,128)(2,1)} %pressure_ref.1), custom_call_target="tpu_custom_call" | custom-call | tf_op jit(solution)/shard_map/pallas_call | solution.py:61
  2.8 13.7 %all-to-all-start = ((bf16[64,64,128]{2,1,0:T(8,128)(2,1)}), bf16[64,64,128]{2,1,0:T(8,128)(2,1)S(1)}, u32[]{:S(2)}, u32[]{:S(2)}) async-start(bf16[64,64,128]{2,1,0:T(8,128)(2,1)} %shard_map.78), calls=%async_computation | async-start | bytes 2097152 | tf_op jit(solution)/shard_map/all_to_all | solution.py:237
  16.5 0.0 copy-done
  16.6 2.9 %collective-permute-start.1 = (s32[1,128]{1,0:T(1,128)S(1)}, s32[1,128]{1,0:T(1,128)S(1)}, u32[]{:S(2)}, u32[]{:S(2)}) collective-permute-start(s32[1,128]{1,0:T(1,128)S(1)} %dynamic-slice_bitcast_fusion), channel_id=1, source_target_pairs={{0,32},{32,0},{1,33},{33,1},{2,34},{34,2},{3,35},{35,3},{4,36},{36... | collective-permute-start | bytes 1544 | tf_op jit(solution)/shard_map/ppermute | solution.py:261
  19.4 0.0 copy-done.2
  19.4 3.4 %collective-permute-start = (bf16[128,128]{1,0:T(8,128)(2,1)S(1)}, bf16[128,128]{1,0:T(8,128)(2,1)S(1)}, u32[]{:S(2)}, u32[]{:S(2)}) collective-permute-start(bf16[128,128]{1,0:T(8,128)(2,1)S(1)} %bitcast.21), channel_id=1, source_target_pairs={{0,1},{1,0},{2,3},{3,2},{4,5},{5,4},{6,7},{7,6},{8,9},{9,8},{10,11... | collective-permute-start | bytes 98312 | tf_op jit(solution)/shard_map/ppermute | solution.py:259
  22.9 0.0 copy-done.3
  22.9 0.1 convert_reduce_fusion
  23.1 0.0 copy-start.1
  23.1 1.9 %copy-done.1 = bf16[1,256,6144]{2,1,0:T(8,128)(2,1)S(1)} copy-done((bf16[1,256,6144]{2,1,0:T(8,128)(2,1)S(1)}, bf16[1,256,6144]{2,1,0:T(8,128)(2,1)}, u32[]{:S(2)}) %copy-start.1) | copy-done | bytes 3145752
  24.9 0.1 shard_map.77.early_ref
  25.1 0.0 collective-permute-done.1
  25.1 15.7 %collective-permute-done.other_ref = bf16[128,128]{1,0:T(8,128)(2,1)S(1)} collective-permute-done((bf16[128,128]{1,0:T(8,128)(2,1)S(1)}, bf16[128,128]{1,0:T(8,128)(2,1)S(1)}, u32[]{:S(2)}, u32[]{:S(2)}) %collective-permute-start) | collective-permute-done | bytes 32800 | tf_op jit(solution)/shard_map/ppermute | solution.py:259
  40.8 0.1 copy.9.target_ref
  41.0 0.2 all-to-all-done.incoming_ref
  41.1 3.2 %shard_map.79 = bf16[512,128]{1,0:T(8,128)(2,1)S(1)} custom-call(bf16[64,64,128]{2,1,0:T(8,128)(2,1)S(1)} %all-to-all-done.incoming_ref, bf16[256,3072]{1,0:T(8,128)(2,1)S(1)} %shard_map.77.early_ref, bf16[256,6144]{1,0:T(8,128)(2,1)} %bitcast.15, s32[1,256]{1,0:T(1,128)S(1)} %multiply_add_fusion.slot_ref, s32[256,1]{1,0:T(8,128)S(1)} %copy.9.target_ref), custom_call_target="tpu_custom_call" | custom-call | tf_op jit(solution)/shard_map/pallas_call | solution.py:138
  44.4 17.8 %all_to_all.21 = bf16[32,16,128]{2,1,0:T(8,128)(2,1)S(1)} all-to-all(bf16[32,16,128]{2,1,0:T(8,128)(2,1)S(1)} %bitcast.17), channel_id=1, replica_groups=mesh['y'=8,'core'=2,'se'=32] {'se'}, dimensions={0} | all-to-all | bytes 262144 | tf_op jit(solution)/shard_map/all_to_all | solution.py:237
  62.2 0.9 shard_map.80
  63.1 4.7 %collective-permute-start.2 = (bf16[32,128]{1,0:T(8,128)(2,1)S(1)}, bf16[32,128]{1,0:T(8,128)(2,1)S(1)}, u32[]{:S(2)}, u32[]{:S(2)}) collective-permute-start(bf16[32,128]{1,0:T(8,128)(2,1)S(1)} %get-tuple-element.15.mine_ref), channel_id=1, source_target_pairs={{0,32},{32,0},{1,33},{33,1},{2,34},{34,2},{3,35},{35,3},{4,36},{36... | collective-permute-start | bytes 24584 | tf_op jit(solution)/shard_map/ppermute | solution.py:269
  67.8 0.8 collective-permute-done.2.theirs_ref
  68.6 0.4 shard_map.81
  69.1 24.9 %all_to_all.22 = bf16[256,2,128]{2,1,0:T(2,128)(2,1)S(1)} all-to-all(bf16[256,2,128]{2,1,0:T(2,128)(2,1)S(1)} %bitcast.19), channel_id=1, replica_groups=mesh['y'=8,'core'=2,'se'=32] {'y','se'}, dimensions={0} | all-to-all | bytes 262144 | tf_op jit(solution)/shard_map/all_to_all | solution.py:237
  93.9 0.7 shard_map.82
  (5 shorter events, 0.1 us)
Async XLA Ops:
  0.6 15.9 %copy-start = (s32[1,16,128]{2,1,0:T(8,128)S(1)}, s32[1,16,128]{2,1,0:T(8,128)}, u32[]{:S(2)}) copy-start(s32[1,16,128]{2,1,0:T(8,128)} %param.11) | copy-start | bytes 24580
  0.6 18.8 %copy-start.2 = (bf16[1,128,128]{2,1,0:T(8,128)(2,1)S(1)}, bf16[1,128,128]{2,1,0:T(8,128)(2,1)}, u32[]{:S(2)}) copy-start(bf16[1,128,128]{2,1,0:T(8,128)(2,1)} %param.10) | copy-start | bytes 98308
  0.7 22.2 %copy-start.3 = (s32[1,256]{1,0:T(1,128)S(1)}, s32[1,256]{1,0:T(1,128)}, u32[]{:S(2)}) copy-start(s32[1,256]{1,0:T(1,128)} %param.9) | copy-start | bytes 3076
  2.8 38.4 %all-to-all-start = ((bf16[64,64,128]{2,1,0:T(8,128)(2,1)}), bf16[64,64,128]{2,1,0:T(8,128)(2,1)S(1)}, u32[]{:S(2)}, u32[]{:S(2)}) async-start(bf16[64,64,128]{2,1,0:T(8,128)(2,1)} %shard_map.78), calls=%async_computation | async-start | bytes 2097152 | tf_op jit(solution)/shard_map/all_to_all | solution.py:237
  16.6 8.6 %collective-permute-start.1 = (s32[1,128]{1,0:T(1,128)S(1)}, s32[1,128]{1,0:T(1,128)S(1)}, u32[]{:S(2)}, u32[]{:S(2)}) collective-permute-start(s32[1,128]{1,0:T(1,128)S(1)} %dynamic-slice_bitcast_fusion), channel_id=1, source_target_pairs={{0,32},{32,0},{1,33},{33,1},{2,34},{34,2},{3,35},{35,3},{4,36},{36... | collective-permute-start | bytes 1544 | tf_op jit(solution)/shard_map/ppermute | solution.py:261
  19.4 21.4 %collective-permute-start = (bf16[128,128]{1,0:T(8,128)(2,1)S(1)}, bf16[128,128]{1,0:T(8,128)(2,1)S(1)}, u32[]{:S(2)}, u32[]{:S(2)}) collective-permute-start(bf16[128,128]{1,0:T(8,128)(2,1)S(1)} %bitcast.21), channel_id=1, source_target_pairs={{0,1},{1,0},{2,3},{3,2},{4,5},{5,4},{6,7},{7,6},{8,9},{9,8},{10,11... | collective-permute-start | bytes 98312 | tf_op jit(solution)/shard_map/ppermute | solution.py:259
  23.1 1.9 %copy-start.1 = (bf16[1,256,6144]{2,1,0:T(8,128)(2,1)S(1)}, bf16[1,256,6144]{2,1,0:T(8,128)(2,1)}, u32[]{:S(2)}) copy-start(bf16[1,256,6144]{2,1,0:T(8,128)(2,1)} %param.8) | copy-start | bytes 9437188
  63.1 5.5 %collective-permute-start.2 = (bf16[32,128]{1,0:T(8,128)(2,1)S(1)}, bf16[32,128]{1,0:T(8,128)(2,1)S(1)}, u32[]{:S(2)}, u32[]{:S(2)}) collective-permute-start(bf16[32,128]{1,0:T(8,128)(2,1)S(1)} %get-tuple-element.15.mine_ref), channel_id=1, source_target_pairs={{0,32},{32,0},{1,33},{33,1},{2,34},{34,2},{3,35},{35,3},{4,36},{36... | collective-permute-start | bytes 24584 | tf_op jit(solution)/shard_map/ppermute | solution.py:269

commit v9 on v8

--- a/solution.py
+++ b/solution.py
@@ -204,7 +204,8 @@
     )(key, mine, theirs)
 
 
-def last_kernel(shares_ref, out_ref):
+def last_kernel(shares_ref, load_ref, out_ref, load_out_ref):
+    load_out_ref[...] = load_ref[...]
     columns, cases = out_ref.shape
     parts = cases // 2
     share = LANES // parts
@@ -223,14 +224,17 @@
             out_ref[i * share + k : i * share + k + 1, :] = both[i : i + 1]
 
 
-def last_sum(shares, columns, cases):
+def last_sum(shares, load, columns):
     return pl.pallas_call(
         last_kernel,
-        out_shape=jax.ShapeDtypeStruct((columns, cases), F32),
-        in_specs=[VMEM],
-        out_specs=VMEM,
+        out_shape=(
+            jax.ShapeDtypeStruct((columns, load.shape[0]), F32),
+            jax.ShapeDtypeStruct(load.shape, F32),
+        ),
+        in_specs=[VMEM, VMEM],
+        out_specs=(VMEM, VMEM),
         compiler_params=LIMIT,
-    )(shares)
+    )(shares, load)
 
 
 def exchange(x, axis):
@@ -265,13 +269,13 @@
 
     packed = condense(incoming, early, level_one[0], slot[None, :], target[:, None], members)
     received = exchange(packed.reshape(members, RC, LANES), "se").reshape(members * RC, LANES)
-    level_two_load, second = assemble(side, received, level_two[0], partner, cases)
+    load, second = assemble(side, received, level_two[0], partner, cases)
     theirs = lax.ppermute(second, "core", [(0, 1), (1, 0)])
     columns = span // members
     share = root_sum(key, second, theirs, groups // 2 * span * (cases // 2) // LANES)
     share = exchange(share, ("y", "se"))
-    root_load = last_sum(share, columns, cases).T
-    return (level_two_load[None], root_load)
+    root_load, level_two_load = last_sum(share, load, columns)
+    return (level_two_load[None], root_load.T)
 
 
 def solution(mesh):

time: 95.1 us -> 94.6 us (level)
  no operation moved by 1% of the time
where the time goes in v9:
time: 94.6 us; the launch traced here: 94.2 us
  blocking collectives  42.7 us (45%)
  starting transfers between devices  24.7 us (26%)
  waiting for transfers between devices  16.7 us (18%)
  Pallas kernels  6.99 us (7%)
  local copies, waits for them, and re-layouts  2.04 us (2%)
    all_to_all x2, blocking collectives, exchange(): return lax.all_to_all(x, axis, split_axis=0, concat_axis=0, tiled=True)  42.7 us
    ppermute x1, waiting for transfers between devices, local(): lax.ppermute(level_two[0], 'se', [(i, i ^ 1) for i in range(members)])  15.7 us
    all_to_all x1, starting transfers between devices, exchange(): return lax.all_to_all(x, axis, split_axis=0, concat_axis=0, tiled=True)  13.7 us
    ppermute x1, starting transfers between devices, local(): theirs = lax.ppermute(second, 'core', [(0, 1), (1, 0)])  4.7 us
    ppermute x1, starting transfers between devices, local(): lax.ppermute(level_two[0], 'se', [(i, i ^ 1) for i in range(members)])  3.42 us
    pallas_call x1, Pallas kernels, condense(): pl.pallas_call(condense_kernel, out_shape=jax.ShapeDtypeStruct((members *...  3.24 us
    ppermute x1, starting transfers between devices, local(): lax.ppermute(root, 'core', [(0, 1), (1, 0)])  2.86 us
    pallas_call x1, Pallas kernels, pack(): pl.pallas_call(pack_kernel, out_shape=jax.ShapeDtypeStruct((members * CAP...  2.1 us
  transfers between devices with their start and end apart: 4, of which 3 were waited for; matrix products, arithmetic and copies ran while one was open for 0% of the time, Pallas kernels for 0%

profile of v9, /device:TPU:1, one launch (start us, length us, event | category | flops | bytes accessed | tf_op | source)
XLA Modules:
  0.0 94.2 jit_solution(17525736912540891783)
XLA Ops:
  0.6 0.0 copy-start
  0.6 0.0 copy-start.2
  0.7 0.0 copy-start.3
  0.7 2.1 %shard_map.78 = bf16[64,64,128]{2,1,0:T(8,128)(2,1)} custom-call(s32[24]{0:T(128)} %owner_ref.1, bf16[24,64,128]{2,1,0:T(8,128)(2,1)} %pressure_ref.1), custom_call_target="tpu_custom_call" | custom-call | tf_op jit(solution)/shard_map/pallas_call | solution.py:61
  2.8 13.7 %all-to-all-start = ((bf16[64,64,128]{2,1,0:T(8,128)(2,1)}), bf16[64,64,128]{2,1,0:T(8,128)(2,1)S(1)}, u32[]{:S(2)}, u32[]{:S(2)}) async-start(bf16[64,64,128]{2,1,0:T(8,128)(2,1)} %shard_map.78), calls=%async_computation | async-start | bytes 2097152 | tf_op jit(solution)/shard_map/all_to_all | solution.py:241
  16.5 0.0 copy-done
  16.6 2.9 %collective-permute-start.1 = (s32[1,128]{1,0:T(1,128)S(1)}, s32[1,128]{1,0:T(1,128)S(1)}, u32[]{:S(2)}, u32[]{:S(2)}) collective-permute-start(s32[1,128]{1,0:T(1,128)S(1)} %dynamic-slice_bitcast_fusion), channel_id=1, source_target_pairs={{0,32},{32,0},{1,33},{33,1},{2,34},{34,2},{3,35},{35,3},{4,36},{36... | collective-permute-start | bytes 1544 | tf_op jit(solution)/shard_map/ppermute | solution.py:265
  19.4 0.0 copy-done.2
  19.4 3.4 %collective-permute-start = (bf16[128,128]{1,0:T(8,128)(2,1)S(1)}, bf16[128,128]{1,0:T(8,128)(2,1)S(1)}, u32[]{:S(2)}, u32[]{:S(2)}) collective-permute-start(bf16[128,128]{1,0:T(8,128)(2,1)S(1)} %bitcast.21), channel_id=1, source_target_pairs={{0,1},{1,0},{2,3},{3,2},{4,5},{5,4},{6,7},{7,6},{8,9},{9,8},{10,11... | collective-permute-start | bytes 98312 | tf_op jit(solution)/shard_map/ppermute | solution.py:263
  22.9 0.0 copy-done.3
  22.9 0.1 convert_reduce_fusion
  23.0 0.0 copy-start.1
  23.1 1.9 %copy-done.1 = bf16[1,256,6144]{2,1,0:T(8,128)(2,1)S(1)} copy-done((bf16[1,256,6144]{2,1,0:T(8,128)(2,1)S(1)}, bf16[1,256,6144]{2,1,0:T(8,128)(2,1)}, u32[]{:S(2)}) %copy-start.1) | copy-done | bytes 3145752
  24.9 0.1 shard_map.77.early_ref
  25.1 0.0 collective-permute-done.1
  25.1 15.7 %collective-permute-done.other_ref = bf16[128,128]{1,0:T(8,128)(2,1)S(1)} collective-permute-done((bf16[128,128]{1,0:T(8,128)(2,1)S(1)}, bf16[128,128]{1,0:T(8,128)(2,1)S(1)}, u32[]{:S(2)}, u32[]{:S(2)}) %collective-permute-start) | collective-permute-done | bytes 32800 | tf_op jit(solution)/shard_map/ppermute | solution.py:263
  40.8 0.1 copy.9.target_ref
  40.9 0.2 all-to-all-done.incoming_ref
  41.1 3.2 %shard_map.79 = bf16[512,128]{1,0:T(8,128)(2,1)S(1)} custom-call(bf16[64,64,128]{2,1,0:T(8,128)(2,1)S(1)} %all-to-all-done.incoming_ref, bf16[256,3072]{1,0:T(8,128)(2,1)S(1)} %shard_map.77.early_ref, bf16[256,6144]{1,0:T(8,128)(2,1)} %bitcast.15, s32[1,256]{1,0:T(1,128)S(1)} %multiply_add_fusion.slot_ref, s32[256,1]{1,0:T(8,128)S(1)} %copy.9.target_ref), custom_call_target="tpu_custom_call" | custom-call | tf_op jit(solution)/shard_map/pallas_call | solution.py:138
  44.4 17.8 %all_to_all.21 = bf16[32,16,128]{2,1,0:T(8,128)(2,1)S(1)} all-to-all(bf16[32,16,128]{2,1,0:T(8,128)(2,1)S(1)} %bitcast.17), channel_id=1, replica_groups=mesh['y'=8,'core'=2,'se'=32] {'se'}, dimensions={0} | all-to-all | bytes 262144 | tf_op jit(solution)/shard_map/all_to_all | solution.py:241
  62.2 0.4 shard_map.80
  62.7 4.7 %collective-permute-start.2 = (bf16[32,128]{1,0:T(8,128)(2,1)S(1)}, bf16[32,128]{1,0:T(8,128)(2,1)S(1)}, u32[]{:S(2)}, u32[]{:S(2)}) collective-permute-start(bf16[32,128]{1,0:T(8,128)(2,1)S(1)} %get-tuple-element.16.mine_ref), channel_id=1, source_target_pairs={{0,32},{32,0},{1,33},{33,1},{2,34},{34,2},{3,35},{35,3},{4,36},{36... | collective-permute-start | bytes 24584 | tf_op jit(solution)/shard_map/ppermute | solution.py:273
  67.4 0.8 collective-permute-done.2.theirs_ref
  68.2 0.4 shard_map.81
  68.6 24.9 %all_to_all.22 = bf16[256,2,128]{2,1,0:T(2,128)(2,1)S(1)} all-to-all(bf16[256,2,128]{2,1,0:T(2,128)(2,1)S(1)} %bitcast.20), channel_id=1, replica_groups=mesh['y'=8,'core'=2,'se'=32] {'y','se'}, dimensions={0} | all-to-all | bytes 262144 | tf_op jit(solution)/shard_map/all_to_all | solution.py:241
  93.5 0.7 shard_map.82
  (5 shorter events, 0.1 us)
Async XLA Ops:
  0.6 15.9 %copy-start = (s32[1,16,128]{2,1,0:T(8,128)S(1)}, s32[1,16,128]{2,1,0:T(8,128)}, u32[]{:S(2)}) copy-start(s32[1,16,128]{2,1,0:T(8,128)} %param.11) | copy-start | bytes 24580
  0.6 18.8 %copy-start.2 = (bf16[1,128,128]{2,1,0:T(8,128)(2,1)S(1)}, bf16[1,128,128]{2,1,0:T(8,128)(2,1)}, u32[]{:S(2)}) copy-start(bf16[1,128,128]{2,1,0:T(8,128)(2,1)} %param.10) | copy-start | bytes 98308
  0.7 22.2 %copy-start.3 = (s32[1,256]{1,0:T(1,128)S(1)}, s32[1,256]{1,0:T(1,128)}, u32[]{:S(2)}) copy-start(s32[1,256]{1,0:T(1,128)} %param.9) | copy-start | bytes 3076
  2.8 38.4 %all-to-all-start = ((bf16[64,64,128]{2,1,0:T(8,128)(2,1)}), bf16[64,64,128]{2,1,0:T(8,128)(2,1)S(1)}, u32[]{:S(2)}, u32[]{:S(2)}) async-start(bf16[64,64,128]{2,1,0:T(8,128)(2,1)} %shard_map.78), calls=%async_computation | async-start | bytes 2097152 | tf_op jit(solution)/shard_map/all_to_all | solution.py:241
  16.6 8.5 %collective-permute-start.1 = (s32[1,128]{1,0:T(1,128)S(1)}, s32[1,128]{1,0:T(1,128)S(1)}, u32[]{:S(2)}, u32[]{:S(2)}) collective-permute-start(s32[1,128]{1,0:T(1,128)S(1)} %dynamic-slice_bitcast_fusion), channel_id=1, source_target_pairs={{0,32},{32,0},{1,33},{33,1},{2,34},{34,2},{3,35},{35,3},{4,36},{36... | collective-permute-start | bytes 1544 | tf_op jit(solution)/shard_map/ppermute | solution.py:265
  19.4 21.4 %collective-permute-start = (bf16[128,128]{1,0:T(8,128)(2,1)S(1)}, bf16[128,128]{1,0:T(8,128)(2,1)S(1)}, u32[]{:S(2)}, u32[]{:S(2)}) collective-permute-start(bf16[128,128]{1,0:T(8,128)(2,1)S(1)} %bitcast.21), channel_id=1, source_target_pairs={{0,1},{1,0},{2,3},{3,2},{4,5},{5,4},{6,7},{7,6},{8,9},{9,8},{10,11... | collective-permute-start | bytes 98312 | tf_op jit(solution)/shard_map/ppermute | solution.py:263
  23.0 1.9 %copy-start.1 = (bf16[1,256,6144]{2,1,0:T(8,128)(2,1)S(1)}, bf16[1,256,6144]{2,1,0:T(8,128)(2,1)}, u32[]{:S(2)}) copy-start(bf16[1,256,6144]{2,1,0:T(8,128)(2,1)} %param.8) | copy-start | bytes 9437188
  62.7 5.5 %collective-permute-start.2 = (bf16[32,128]{1,0:T(8,128)(2,1)S(1)}, bf16[32,128]{1,0:T(8,128)(2,1)S(1)}, u32[]{:S(2)}, u32[]{:S(2)}) collective-permute-start(bf16[32,128]{1,0:T(8,128)(2,1)S(1)} %get-tuple-element.16.mine_ref), channel_id=1, source_target_pairs={{0,32},{32,0},{1,33},{33,1},{2,34},{34,2},{3,35},{35,3},{4,36},{36... | collective-permute-start | bytes 24584 | tf_op jit(solution)/shard_map/ppermute | solution.py:273

commit v10 on v5

--- a/solution.py
+++ b/solution.py
@@ -117,9 +117,12 @@
     other = jnp.where((lane >= cases) & (lane < cases + parts), other, 0.0)
     other = jnp.where(lane == cases + parts + 1, offset, other)
     slot = slot_ref[...]
-    want = iota((out_ref.shape[0], slot.shape[1]), 0)
-    sent = jnp.dot(one_hot(slot == want), own.astype(BF16), preferred_element_type=F32)
-    sent += jnp.dot(one_hot(slot == want ^ RC), other.astype(BF16), preferred_element_type=F32)
+    choose = one_hot(slot == iota((out_ref.shape[0], slot.shape[1]), 0))
+    both = jnp.concatenate([own, other], axis=1).astype(BF16)
+    chosen = jnp.dot(choose, both, preferred_element_type=F32)
+    blocks = chosen[:, LANES : 2 * LANES].reshape(-1, 2, RC, LANES)
+    swapped = jnp.concatenate([blocks[:, 1:2], blocks[:, 0:1]], axis=1)
+    sent = chosen[:, 0:LANES] + swapped.reshape(-1, LANES)
     out_ref[...] = sent.astype(BF16)
 
 
@@ -146,8 +149,10 @@
     rows = rows_ref[...]
     offsets = rows.astype(F32)[:, cases + parts : cases + parts + 2]
     want = (iota(rows.shape, 1) + 1).astype(F32)
-    load = dot_tn(rows, one_hot(offsets[:, 0:1] == want))[0:cases]
-    other = dot_tn(rows, one_hot(offsets[:, 1:2] == want))[cases : cases + parts]
+    hits = jnp.concatenate([one_hot(offsets[:, 0:1] == want), one_hot(offsets[:, 1:2] == want)], axis=1)
+    loads = dot_tn(rows, hits)
+    load = loads[0:cases, 0:LANES]
+    other = loads[cases : cases + parts, LANES : 2 * LANES]
     load_ref[...] = load
     second = dot_nt(load.astype(BF16), matrix_ref[...])
     second = jnp.where(side_ref[0] == 0, second[0:parts], second[parts:cases])
@@ -193,7 +198,8 @@
     )(key, mine, theirs)
 
 
-def last_kernel(shares_ref, out_ref):
+def last_kernel(shares_ref, load_ref, out_ref, load_out_ref):
+    load_out_ref[...] = load_ref[...]
     columns, cases = out_ref.shape
     parts = cases // 2
     share = LANES // parts
@@ -212,14 +218,17 @@
             out_ref[i * share + k : i * share + k + 1, :] = both[i : i + 1]
 
 
-def last_sum(shares, columns, cases):
+def last_sum(shares, load, columns):
     return pl.pallas_call(
         last_kernel,
-        out_shape=jax.ShapeDtypeStruct((columns, cases), F32),
-        in_specs=[VMEM],
-        out_specs=VMEM,
+        out_shape=(
+            jax.ShapeDtypeStruct((columns, load.shape[0]), F32),
+            jax.ShapeDtypeStruct(load.shape, F32),
+        ),
+        in_specs=[VMEM, VMEM],
+        out_specs=(VMEM, VMEM),
         compiler_params=LIMIT,
-    )(shares)
+    )(shares, load)
 
 
 def exchange(x, axis):
@@ -249,17 +258,17 @@
     roots = jnp.concatenate([root, lax.ppermute(root, "core", [(0, 1), (1, 0)])], axis=0)
     group = roots // span
     key = jnp.where(group % 2 == core, group // 2 * span + roots % span, -1)
-    target, partner, key = lax.optimization_barrier((target, partner, key))
+    target, partner, key, side = lax.optimization_barrier((target, partner, key, side))
 
     packed = condense(incoming, level_one[0], slot[None, :], target[:, None], members)
     received = exchange(packed.reshape(members, RC, LANES), "se").reshape(members * RC, LANES)
-    level_two_load, second = assemble(side, received, level_two[0], partner, cases)
+    load, second = assemble(side, received, level_two[0], partner, cases)
     theirs = lax.ppermute(second, "core", [(0, 1), (1, 0)])
     columns = span // members
     share = root_sum(key, second, theirs, groups // 2 * span * (cases // 2) // LANES)
     share = exchange(share, ("y", "se"))
-    root_load = last_sum(share, columns, cases).T
-    return (level_two_load[None], root_load)
+    root_load, level_two_load = last_sum(share, load, columns)
+    return (level_two_load[None], root_load.T)
 
 
 def solution(mesh):

time: 96.2 us -> 94.7 us (0.984)
  blocking collectives: 24.9 us -> 42.7 us
  waiting for transfers between devices: 27.6 us -> 18.5 us
  starting transfers between devices: 33.9 us -> 25 us
  Pallas kernels: 8.21 us -> 6.88 us
    all_to_all x1 -> x2, blocking collectives: 24.9 us -> 42.7 us  [exchange(): return lax.all_to_all(x, axis, split_axis=0, concat_axis=0, tiled=True)]
    all_to_all x2 -> x1, waiting for transfers between devices: 9.35 us -> 0.18 us  [exchange(): return lax.all_to_all(x, axis, split_axis=0, concat_axis=0, tiled=True)]
    all_to_all x2 -> x1, starting transfers between devices: 22.7 us -> 13.9 us  [exchange(): return lax.all_to_all(x, axis, split_axis=0, concat_axis=0, tiled=True)]
  transfers between devices with their start and end apart: 5 -> 4, of which waited for: 5 -> 4; matrix products, arithmetic and copies ran while one was open for 0% -> 0% of each run, Pallas kernels for 0% -> 0%
where the time goes in v10:
time: 94.7 us; the launch traced here: 94.3 us
  blocking collectives  42.7 us (45%)
  starting transfers between devices  25 us (26%)
  waiting for transfers between devices  18.5 us (20%)
  Pallas kernels  6.88 us (7%)
    all_to_all x2, blocking collectives, exchange(): return lax.all_to_all(x, axis, split_axis=0, concat_axis=0, tiled=True)  42.7 us
    ppermute x1, waiting for transfers between devices, local(): lax.ppermute(level_two[0], 'se', [(i, i ^ 1) for i in range(members)])  16.9 us
    all_to_all x1, starting transfers between devices, exchange(): return lax.all_to_all(x, axis, split_axis=0, concat_axis=0, tiled=True)  13.9 us
    ppermute x1, starting transfers between devices, local(): theirs = lax.ppermute(second, 'core', [(0, 1), (1, 0)])  4.69 us
    ppermute x1, starting transfers between devices, local(): lax.ppermute(root, 'core', [(0, 1), (1, 0)])  3.42 us
    ppermute x1, starting transfers between devices, local(): lax.ppermute(level_two[0], 'se', [(i, i ^ 1) for i in range(members)])  3.06 us
    pallas_call x1, Pallas kernels, condense(): pl.pallas_call(condense_kernel, out_shape=jax.ShapeDtypeStruct((members *...  3.05 us
    pallas_call x1, Pallas kernels, pack(): pl.pallas_call(pack_kernel, out_shape=jax.ShapeDtypeStruct((members * CAP...  2.29 us
  transfers between devices with their start and end apart: 4, of which 4 were waited for; matrix products, arithmetic and copies ran while one was open for 0% of the time, Pallas kernels for 0%

profile of v10, /device:TPU:1, one launch (start us, length us, event | category | flops | bytes accessed | tf_op | source)
XLA Modules:
  0.0 94.3 jit_solution(8997825566070951092)
XLA Ops:
  0.6 0.0 copy-start
  0.6 0.0 copy-start.2
  0.7 0.0 copy-start.3
  0.7 0.0 copy-start.1
  0.7 2.3 %shard_map.78 = bf16[64,64,128]{2,1,0:T(8,128)(2,1)} custom-call(s32[24]{0:T(128)} %owner_ref.1, bf16[24,64,128]{2,1,0:T(8,128)(2,1)} %pressure_ref.1), custom_call_target="tpu_custom_call" | custom-call | tf_op jit(solution)/shard_map/pallas_call | solution.py:60
  3.0 13.9 %all-to-all-start = ((bf16[64,64,128]{2,1,0:T(8,128)(2,1)}), bf16[64,64,128]{2,1,0:T(8,128)(2,1)}, u32[]{:S(2)}, u32[]{:S(2)}) async-start(bf16[64,64,128]{2,1,0:T(8,128)(2,1)} %shard_map.78), calls=%async_computation | async-start | bytes 2097152 | tf_op jit(solution)/shard_map/all_to_all | solution.py:235
  16.8 0.0 copy-done.2
  16.8 3.1 %collective-permute-start = (bf16[128,128]{1,0:T(8,128)(2,1)S(1)}, bf16[128,128]{1,0:T(8,128)(2,1)S(1)}, u32[]{:S(2)}, u32[]{:S(2)}) collective-permute-start(bf16[128,128]{1,0:T(8,128)(2,1)S(1)} %bitcast.21), channel_id=1, source_target_pairs={{0,1},{1,0},{2,3},{3,2},{4,5},{5,4},{6,7},{7,6},{8,9},{9,8},{10,11... | collective-permute-start | bytes 98312 | tf_op jit(solution)/shard_map/ppermute | solution.py:256
  19.9 0.0 copy-done
  20.0 3.4 %collective-permute-start.1 = (s32[1,128]{1,0:T(1,128)S(1)}, s32[1,128]{1,0:T(1,128)S(1)}, u32[]{:S(2)}, u32[]{:S(2)}) collective-permute-start(s32[1,128]{1,0:T(1,128)S(1)} %dynamic-slice_bitcast_fusion), channel_id=1, source_target_pairs={{0,32},{32,0},{1,33},{33,1},{2,34},{34,2},{3,35},{35,3},{4,36},{36... | collective-permute-start | bytes 1544 | tf_op jit(solution)/shard_map/ppermute | solution.py:258
  23.4 0.0 copy-done.3
  23.4 0.0 copy-done.1
  23.5 0.1 convert_reduce_fusion
  23.6 0.6 collective-permute-done.1
  24.2 16.9 %collective-permute-done.other_ref = bf16[128,128]{1,0:T(8,128)(2,1)S(1)} collective-permute-done((bf16[128,128]{1,0:T(8,128)(2,1)S(1)}, bf16[128,128]{1,0:T(8,128)(2,1)S(1)}, u32[]{:S(2)}, u32[]{:S(2)}) %collective-permute-start) | collective-permute-done | bytes 32800 | tf_op jit(solution)/shard_map/ppermute | solution.py:256
  41.1 0.1 copy.9.target_ref
  41.3 0.2 all-to-all-done.arrived_ref
  41.4 3.0 %shard_map.79 = bf16[512,128]{1,0:T(8,128)(2,1)S(1)} custom-call(bf16[64,64,128]{2,1,0:T(8,128)(2,1)} %all-to-all-done.arrived_ref, bf16[256,6144]{1,0:T(8,128)(2,1)S(1)} %bitcast.16, s32[1,256]{1,0:T(1,128)S(1)} %multiply_add_fusion.slot_ref, s32[256,1]{1,0:T(8,128)S(1)} %copy.9.target_ref), custom_call_target="tpu_custom_call" | custom-call | tf_op jit(solution)/shard_map/pallas_call | solution.py:132
  44.5 17.9 %all_to_all.21 = bf16[32,16,128]{2,1,0:T(8,128)(2,1)S(1)} all-to-all(bf16[32,16,128]{2,1,0:T(8,128)(2,1)S(1)} %bitcast.17), channel_id=1, replica_groups=mesh['y'=8,'core'=2,'se'=32] {'se'}, dimensions={0} | all-to-all | bytes 262144 | tf_op jit(solution)/shard_map/all_to_all | solution.py:235
  62.4 0.4 shard_map.80
  62.8 4.7 %collective-permute-start.2 = (bf16[32,128]{1,0:T(8,128)(2,1)S(1)}, bf16[32,128]{1,0:T(8,128)(2,1)S(1)}, u32[]{:S(2)}, u32[]{:S(2)}) collective-permute-start(bf16[32,128]{1,0:T(8,128)(2,1)S(1)} %get-tuple-element.14.mine_ref), channel_id=1, source_target_pairs={{0,32},{32,0},{1,33},{33,1},{2,34},{34,2},{3,35},{35,3},{4,36},{36... | collective-permute-start | bytes 24584 | tf_op jit(solution)/shard_map/ppermute | solution.py:266
  67.5 0.8 collective-permute-done.2.theirs_ref
  68.3 0.4 shard_map.81
  68.7 24.9 %all_to_all.22 = bf16[256,2,128]{2,1,0:T(2,128)(2,1)S(1)} all-to-all(bf16[256,2,128]{2,1,0:T(2,128)(2,1)S(1)} %bitcast.20), channel_id=1, replica_groups=mesh['y'=8,'core'=2,'se'=32] {'y','se'}, dimensions={0} | all-to-all | bytes 262144 | tf_op jit(solution)/shard_map/all_to_all | solution.py:235
  93.6 0.7 shard_map.82
  (6 shorter events, 0.1 us)
Async XLA Ops:
  0.6 19.3 %copy-start = (s32[1,16,128]{2,1,0:T(8,128)S(1)}, s32[1,16,128]{2,1,0:T(8,128)}, u32[]{:S(2)}) copy-start(s32[1,16,128]{2,1,0:T(8,128)} %param.11) | copy-start | bytes 24580
  0.6 16.2 %copy-start.2 = (bf16[1,128,128]{2,1,0:T(8,128)(2,1)S(1)}, bf16[1,128,128]{2,1,0:T(8,128)(2,1)}, u32[]{:S(2)}) copy-start(bf16[1,128,128]{2,1,0:T(8,128)(2,1)} %param.10) | copy-start | bytes 98308
  0.7 22.7 %copy-start.3 = (s32[1,256]{1,0:T(1,128)S(1)}, s32[1,256]{1,0:T(1,128)}, u32[]{:S(2)}) copy-start(s32[1,256]{1,0:T(1,128)} %target_ref.1) | copy-start | bytes 3076
  0.7 22.7 %copy-start.1 = (bf16[1,256,6144]{2,1,0:T(8,128)(2,1)S(1)}, bf16[1,256,6144]{2,1,0:T(8,128)(2,1)}, u32[]{:S(2)}) copy-start(bf16[1,256,6144]{2,1,0:T(8,128)(2,1)} %param.8) | copy-start | bytes 9437188
  3.0 38.5 %all-to-all-start = ((bf16[64,64,128]{2,1,0:T(8,128)(2,1)}), bf16[64,64,128]{2,1,0:T(8,128)(2,1)}, u32[]{:S(2)}, u32[]{:S(2)}) async-start(bf16[64,64,128]{2,1,0:T(8,128)(2,1)} %shard_map.78), calls=%async_computation | async-start | bytes 2097152 | tf_op jit(solution)/shard_map/all_to_all | solution.py:235
  16.8 24.3 %collective-permute-start = (bf16[128,128]{1,0:T(8,128)(2,1)S(1)}, bf16[128,128]{1,0:T(8,128)(2,1)S(1)}, u32[]{:S(2)}, u32[]{:S(2)}) collective-permute-start(bf16[128,128]{1,0:T(8,128)(2,1)S(1)} %bitcast.21), channel_id=1, source_target_pairs={{0,1},{1,0},{2,3},{3,2},{4,5},{5,4},{6,7},{7,6},{8,9},{9,8},{10,11... | collective-permute-start | bytes 98312 | tf_op jit(solution)/shard_map/ppermute | solution.py:256
  20.0 4.2 %collective-permute-start.1 = (s32[1,128]{1,0:T(1,128)S(1)}, s32[1,128]{1,0:T(1,128)S(1)}, u32[]{:S(2)}, u32[]{:S(2)}) collective-permute-start(s32[1,128]{1,0:T(1,128)S(1)} %dynamic-slice_bitcast_fusion), channel_id=1, source_target_pairs={{0,32},{32,0},{1,33},{33,1},{2,34},{34,2},{3,35},{35,3},{4,36},{36... | collective-permute-start | bytes 1544 | tf_op jit(solution)/shard_map/ppermute | solution.py:258
  62.8 5.5 %collective-permute-start.2 = (bf16[32,128]{1,0:T(8,128)(2,1)S(1)}, bf16[32,128]{1,0:T(8,128)(2,1)S(1)}, u32[]{:S(2)}, u32[]{:S(2)}) collective-permute-start(bf16[32,128]{1,0:T(8,128)(2,1)S(1)} %get-tuple-element.14.mine_ref), channel_id=1, source_target_pairs={{0,32},{32,0},{1,33},{33,1},{2,34},{34,2},{3,35},{35,3},{4,36},{36... | collective-permute-start | bytes 24584 | tf_op jit(solution)/shard_map/ppermute | solution.py:266

commit v11 on v9

--- a/solution.py
+++ b/solution.py
@@ -41,15 +41,21 @@
 def pack_kernel(owner_ref, pressure_ref, out_ref, held_ref, owner_smem, count_ref, owner_sem, block_sem):
     slots = out_ref.shape[0]
     owners = pltpu.make_async_copy(owner_ref, owner_smem, owner_sem)
-    blocks = pltpu.make_async_copy(pressure_ref, held_ref, block_sem)
+    half = held_ref.shape[0] // 2
+    halves = []
+    for h in range(2):
+        part = slice(h * half, held_ref.shape[0] if h else half)
+        halves.append(pltpu.make_async_copy(pressure_ref.at[part], held_ref.at[part], block_sem.at[h]))
     owners.start()
-    blocks.start()
+    for copy in halves:
+        copy.start()
     out_ref[:, 0:16, :] = jnp.full((slots, 16, out_ref.shape[2]), EMPTY, BF16)
     for e in range(slots // CAPACITY):
         count_ref[e] = 0
     owners.wait()
-    blocks.wait()
     for t in range(held_ref.shape[0]):
+        if t == 0 or t == half:
+            halves[t // half].wait()
         owner = owner_smem[t]
         count = count_ref[owner]
         count_ref[owner] = count + 1
@@ -68,7 +74,7 @@
             pltpu.SMEM((blocks,), I32),
             pltpu.SMEM((members,), I32),
             pltpu.SemaphoreType.DMA,
-            pltpu.SemaphoreType.DMA,
+            pltpu.SemaphoreType.DMA((2,)),
         ],
         compiler_params=WIDE,
     )(block_owner, pressure)

time: 94.6 us -> 94.6 us (level)
  no operation moved by 1% of the time
where the time goes in v11:
time: 94.6 us; the launch traced here: 94.1 us
  blocking collectives  42.8 us (45%)
  starting transfers between devices  24.6 us (26%)
  waiting for transfers between devices  16.7 us (18%)
  Pallas kernels  6.97 us (7%)
  local copies, waits for them, and re-layouts  2.04 us (2%)
    all_to_all x2, blocking collectives, exchange(): return lax.all_to_all(x, axis, split_axis=0, concat_axis=0, tiled=True)  42.8 us
    ppermute x1, waiting for transfers between devices, local(): lax.ppermute(level_two[0], 'se', [(i, i ^ 1) for i in range(members)])  15.7 us
    all_to_all x1, starting transfers between devices, exchange(): return lax.all_to_all(x, axis, split_axis=0, concat_axis=0, tiled=True)  13.7 us
    ppermute x1, starting transfers between devices, local(): theirs = lax.ppermute(second, 'core', [(0, 1), (1, 0)])  4.64 us
    ppermute x1, starting transfers between devices, local(): lax.ppermute(level_two[0], 'se', [(i, i ^ 1) for i in range(members)])  3.42 us
    pallas_call x1, Pallas kernels, condense(): pl.pallas_call(condense_kernel, out_shape=jax.ShapeDtypeStruct((members *...  3.24 us
    ppermute x1, starting transfers between devices, local(): lax.ppermute(root, 'core', [(0, 1), (1, 0)])  2.86 us
    pallas_call x1, Pallas kernels, pack(): pl.pallas_call(pack_kernel, out_shape=jax.ShapeDtypeStruct((members * CAP...  2.08 us
  transfers between devices with their start and end apart: 4, of which 3 were waited for; matrix products, arithmetic and copies ran while one was open for 0% of the time, Pallas kernels for 0%

profile of v11, /device:TPU:1, one launch (start us, length us, event | category | flops | bytes accessed | tf_op | source)
XLA Modules:
  0.0 94.1 jit_solution(9507976123866429511)
XLA Ops:
  0.6 0.0 copy-start
  0.6 0.0 copy-start.2
  0.7 0.0 copy-start.3
  0.7 2.1 %shard_map.78 = bf16[64,64,128]{2,1,0:T(8,128)(2,1)} custom-call(s32[24]{0:T(128)} %owner_ref.1, bf16[24,64,128]{2,1,0:T(8,128)(2,1)} %pressure_ref.1), custom_call_target="tpu_custom_call" | custom-call | tf_op jit(solution)/shard_map/pallas_call | solution.py:67
  2.7 13.7 %all-to-all-start = ((bf16[64,64,128]{2,1,0:T(8,128)(2,1)}), bf16[64,64,128]{2,1,0:T(8,128)(2,1)S(1)}, u32[]{:S(2)}, u32[]{:S(2)}) async-start(bf16[64,64,128]{2,1,0:T(8,128)(2,1)} %shard_map.78), calls=%async_computation | async-start | bytes 2097152 | tf_op jit(solution)/shard_map/all_to_all | solution.py:247
  16.5 0.0 copy-done
  16.5 2.9 %collective-permute-start.1 = (s32[1,128]{1,0:T(1,128)S(1)}, s32[1,128]{1,0:T(1,128)S(1)}, u32[]{:S(2)}, u32[]{:S(2)}) collective-permute-start(s32[1,128]{1,0:T(1,128)S(1)} %dynamic-slice_bitcast_fusion), channel_id=1, source_target_pairs={{0,32},{32,0},{1,33},{33,1},{2,34},{34,2},{3,35},{35,3},{4,36},{36... | collective-permute-start | bytes 1544 | tf_op jit(solution)/shard_map/ppermute | solution.py:271
  19.4 0.0 copy-done.2
  19.4 3.4 %collective-permute-start = (bf16[128,128]{1,0:T(8,128)(2,1)S(1)}, bf16[128,128]{1,0:T(8,128)(2,1)S(1)}, u32[]{:S(2)}, u32[]{:S(2)}) collective-permute-start(bf16[128,128]{1,0:T(8,128)(2,1)S(1)} %bitcast.21), channel_id=1, source_target_pairs={{0,1},{1,0},{2,3},{3,2},{4,5},{5,4},{6,7},{7,6},{8,9},{9,8},{10,11... | collective-permute-start | bytes 98312 | tf_op jit(solution)/shard_map/ppermute | solution.py:269
  22.8 0.0 copy-done.3
  22.9 0.1 convert_reduce_fusion
  23.0 0.0 copy-start.1
  23.0 1.9 %copy-done.1 = bf16[1,256,6144]{2,1,0:T(8,128)(2,1)S(1)} copy-done((bf16[1,256,6144]{2,1,0:T(8,128)(2,1)S(1)}, bf16[1,256,6144]{2,1,0:T(8,128)(2,1)}, u32[]{:S(2)}) %copy-start.1) | copy-done | bytes 3145752
  24.9 0.1 shard_map.77.early_ref
  25.1 0.0 collective-permute-done.1
  25.1 15.7 %collective-permute-done.other_ref = bf16[128,128]{1,0:T(8,128)(2,1)S(1)} collective-permute-done((bf16[128,128]{1,0:T(8,128)(2,1)S(1)}, bf16[128,128]{1,0:T(8,128)(2,1)S(1)}, u32[]{:S(2)}, u32[]{:S(2)}) %collective-permute-start) | collective-permute-done | bytes 32800 | tf_op jit(solution)/shard_map/ppermute | solution.py:269
  40.8 0.1 copy.9.target_ref
  40.9 0.2 all-to-all-done.incoming_ref
  41.1 3.2 %shard_map.79 = bf16[512,128]{1,0:T(8,128)(2,1)S(1)} custom-call(bf16[64,64,128]{2,1,0:T(8,128)(2,1)S(1)} %all-to-all-done.incoming_ref, bf16[256,3072]{1,0:T(8,128)(2,1)S(1)} %shard_map.77.early_ref, bf16[256,6144]{1,0:T(8,128)(2,1)} %bitcast.15, s32[1,256]{1,0:T(1,128)S(1)} %multiply_add_fusion.slot_ref, s32[256,1]{1,0:T(8,128)S(1)} %copy.9.target_ref), custom_call_target="tpu_custom_call" | custom-call | tf_op jit(solution)/shard_map/pallas_call | solution.py:144
  44.4 17.9 %all_to_all.21 = bf16[32,16,128]{2,1,0:T(8,128)(2,1)S(1)} all-to-all(bf16[32,16,128]{2,1,0:T(8,128)(2,1)S(1)} %bitcast.17), channel_id=1, replica_groups=mesh['y'=8,'core'=2,'se'=32] {'se'}, dimensions={0} | all-to-all | bytes 262144 | tf_op jit(solution)/shard_map/all_to_all | solution.py:247
  62.2 0.4 shard_map.80
  62.6 4.6 %collective-permute-start.2 = (bf16[32,128]{1,0:T(8,128)(2,1)S(1)}, bf16[32,128]{1,0:T(8,128)(2,1)S(1)}, u32[]{:S(2)}, u32[]{:S(2)}) collective-permute-start(bf16[32,128]{1,0:T(8,128)(2,1)S(1)} %get-tuple-element.16.mine_ref), channel_id=1, source_target_pairs={{0,32},{32,0},{1,33},{33,1},{2,34},{34,2},{3,35},{35,3},{4,36},{36... | collective-permute-start | bytes 24584 | tf_op jit(solution)/shard_map/ppermute | solution.py:279
  67.3 0.8 collective-permute-done.2.theirs_ref
  68.1 0.4 shard_map.81
  68.5 24.9 %all_to_all.22 = bf16[256,2,128]{2,1,0:T(2,128)(2,1)S(1)} all-to-all(bf16[256,2,128]{2,1,0:T(2,128)(2,1)S(1)} %bitcast.20), channel_id=1, replica_groups=mesh['y'=8,'core'=2,'se'=32] {'y','se'}, dimensions={0} | all-to-all | bytes 262144 | tf_op jit(solution)/shard_map/all_to_all | solution.py:247
  93.4 0.7 shard_map.82
  (5 shorter events, 0.1 us)
Async XLA Ops:
  0.6 15.9 %copy-start = (s32[1,16,128]{2,1,0:T(8,128)S(1)}, s32[1,16,128]{2,1,0:T(8,128)}, u32[]{:S(2)}) copy-start(s32[1,16,128]{2,1,0:T(8,128)} %param.11) | copy-start | bytes 24580
  0.6 18.8 %copy-start.2 = (bf16[1,128,128]{2,1,0:T(8,128)(2,1)S(1)}, bf16[1,128,128]{2,1,0:T(8,128)(2,1)}, u32[]{:S(2)}) copy-start(bf16[1,128,128]{2,1,0:T(8,128)(2,1)} %param.10) | copy-start | bytes 98308
  0.7 22.2 %copy-start.3 = (s32[1,256]{1,0:T(1,128)S(1)}, s32[1,256]{1,0:T(1,128)}, u32[]{:S(2)}) copy-start(s32[1,256]{1,0:T(1,128)} %param.9) | copy-start | bytes 3076
  2.7 38.4 %all-to-all-start = ((bf16[64,64,128]{2,1,0:T(8,128)(2,1)}), bf16[64,64,128]{2,1,0:T(8,128)(2,1)S(1)}, u32[]{:S(2)}, u32[]{:S(2)}) async-start(bf16[64,64,128]{2,1,0:T(8,128)(2,1)} %shard_map.78), calls=%async_computation | async-start | bytes 2097152 | tf_op jit(solution)/shard_map/all_to_all | solution.py:247
  16.5 8.5 %collective-permute-start.1 = (s32[1,128]{1,0:T(1,128)S(1)}, s32[1,128]{1,0:T(1,128)S(1)}, u32[]{:S(2)}, u32[]{:S(2)}) collective-permute-start(s32[1,128]{1,0:T(1,128)S(1)} %dynamic-slice_bitcast_fusion), channel_id=1, source_target_pairs={{0,32},{32,0},{1,33},{33,1},{2,34},{34,2},{3,35},{35,3},{4,36},{36... | collective-permute-start | bytes 1544 | tf_op jit(solution)/shard_map/ppermute | solution.py:271
  19.4 21.4 %collective-permute-start = (bf16[128,128]{1,0:T(8,128)(2,1)S(1)}, bf16[128,128]{1,0:T(8,128)(2,1)S(1)}, u32[]{:S(2)}, u32[]{:S(2)}) collective-permute-start(bf16[128,128]{1,0:T(8,128)(2,1)S(1)} %bitcast.21), channel_id=1, source_target_pairs={{0,1},{1,0},{2,3},{3,2},{4,5},{5,4},{6,7},{7,6},{8,9},{9,8},{10,11... | collective-permute-start | bytes 98312 | tf_op jit(solution)/shard_map/ppermute | solution.py:269
  23.0 1.9 %copy-start.1 = (bf16[1,256,6144]{2,1,0:T(8,128)(2,1)S(1)}, bf16[1,256,6144]{2,1,0:T(8,128)(2,1)}, u32[]{:S(2)}) copy-start(bf16[1,256,6144]{2,1,0:T(8,128)(2,1)} %param.8) | copy-start | bytes 9437188
  62.6 5.5 %collective-permute-start.2 = (bf16[32,128]{1,0:T(8,128)(2,1)S(1)}, bf16[32,128]{1,0:T(8,128)(2,1)S(1)}, u32[]{:S(2)}, u32[]{:S(2)}) collective-permute-start(bf16[32,128]{1,0:T(8,128)(2,1)S(1)} %get-tuple-element.16.mine_ref), channel_id=1, source_target_pairs={{0,32},{32,0},{1,33},{33,1},{2,34},{34,2},{3,35},{35,3},{4,36},{36... | collective-permute-start | bytes 24584 | tf_op jit(solution)/shard_map/ppermute | solution.py:279
